TPU v7x, 256 devices: a whole 4x4x8 slice. The times are simulated.
256 devices in a mesh: ctxa: 8 (over z_hi, core), ctxb: 32 (over z_lo, y, x).
Axes of the slice: x: 4, y: 4, z: 8 (z_hi: 4, z_lo: 2; z = z_hi * 2 + z_lo), core: 2. Of those that a mesh axis runs over, the one named last changes fastest.
Arguments:
- queries: bfloat16 [32768, 512], P(('ctxa', 'ctxb')), may hold values from -8 to 8
- keys: bfloat16 [32768, 512], P(('ctxa', 'ctxb')), may hold values from -8 to 8
- values: bfloat16 [32768, 512], P(('ctxa', 'ctxb')), may hold values from -6 to 6
- grad_out: bfloat16 [32768, 512], P(('ctxa', 'ctxb')), may hold values from -48 to 48
- offsets: int32 [3, 8], replicated, may hold values from 0 to 31, as said below
Outputs:
- grad_queries: bfloat16 [32768, 512], P(('ctxa', 'ctxb'))
- grad_keys: bfloat16 [32768, 512], P(('ctxa', 'ctxb'))
- grad_values: bfloat16 [32768, 512], P(('ctxa', 'ctxb'))
Inputs may be any that keep to these rules, and one draw needn't show every extreme that they name: offsets[l, h] is below the dilation of level l; at every level some head has the dilation minus one.
All inputs are finite; a program needn't handle non-finite values.
Results may differ from a plain program's by a relative error of at most 0.0093.
Values may be sent and summed in bfloat16 or wider, within the bound.
A program may use at most 128 MiB of HBM per device.

v0:
```python
import math

import jax
import jax.numpy as jnp
from jax import lax
from jax.experimental import pallas as pl
from jax.experimental.pallas import tpu as pltpu
from jax.sharding import PartitionSpec as P

HEADS = 8
HEAD_DIM = 64
KEYS = 1024
LEVELS = 3
ROWS = 128
HALF = ROWS // 2
GROUP = 8
MATES = 16
WIDE = 512
FEW = 32
TILE = 16
QUARTER = HALF // 2
PAIR = 2 * HEAD_DIM
SCALE = HEAD_DIM ** (-0.5)
TO_EXP2 = SCALE * math.log2(math.e)
LOWEST = -1e30
MESH = pl.DeviceIdType.MESH
F32 = jnp.float32
BF16 = jnp.bfloat16
COLS = 256
SLOTS = COLS // HALF
DEEP = 128


def dot(x, y):
    return jnp.dot(x, y, preferred_element_type=F32)


def dot_nt(x, y):
    return lax.dot_general(x, y, (((1,), (1,)), ((), ())), preferred_element_type=F32)


def iota(shape, dim):
    return lax.broadcasted_iota(jnp.int32, shape, dim)


def one_hot(hit):
    return hit.astype(F32).astype(BF16)


def two_parts(x):
    high = x.astype(BF16)
    return high, (x - high.astype(F32)).astype(BF16)


def fold8(x, op):
    parts = [x[8 * i : 8 * i + 8] for i in range(x.shape[0] // 8)]
    while len(parts) > 1:
        parts = [op(parts[i], parts[i + 1]) for i in range(0, len(parts), 2)]
    return parts[0]


def kernel(
    off_hbm,
    q_hbm,
    k_hbm,
    v_hbm,
    g_hbm,
    out_ref,
    off_ref,
    q_ref,
    k_ref,
    v_ref,
    g_ref,
    send_few,
    send_kv,
    send_qg,
    few,
    kv,
    qg,
    peer,
    keys2,
    kv_k,
    kv_v,
    k_t,
    part1,
    got1,
    part2,
    part2_own,
    sib,
    back2,
    got2,
    out_kv,
    out_q,
    fin_kv,
    fin_q,
    score,
    dprob,
    dsc,
    acc,
    few_sem,
    kv_sem,
    qg_sem,
    l1_sem,
    l2_sem,
    pass_sem,
    b1_sem,
    half_sem,
    b2_sem,
    dq_sem,
    home_sem,
    load_sem,
):
    loads = []
    for i, (src, dst) in enumerate(
        ((k_hbm, k_ref), (v_hbm, v_ref), (q_hbm, q_ref), (g_hbm, g_ref), (off_hbm, off_ref))
    ):
        load = pltpu.make_async_copy(src, dst, load_sem.at[i])
        load.start()
        loads.append(load)

    major = lax.axis_index("ctxa")
    minor = lax.axis_index("ctxb")
    head = minor % GROUP
    mate = (major // 2) * 4 + minor // GROUP

    def member(dx, dy):
        x = (head % 4 + dx) % 4
        y = (head // 4 + dy) % 2
        return y * 4 + x

    def at_head(other):
        return (major, (minor // GROUP) * GROUP + other)

    def at_mate(other):
        return ((other // 4) * 2 + major % 2, (other % 4) * GROUP + head)

    ahead = [member(r % 4, r // 4) for r in range(GROUP)]
    behind = [member(4 - r % 4, r // 4) for r in range(GROUP)]
    sibling = (major + 1 - 2 * (major % 2), minor)
    partner = (major, minor + GROUP - 2 * GROUP * ((minor // GROUP) % 2))

    def remote(src, dst, sems, device):
        return pltpu.make_async_remote_copy(
            src_ref=src,
            dst_ref=dst,
            send_sem=sems[0],
            recv_sem=sems[1],
            device_id=device,
            device_id_type=MESH,
        )

    def pair_of(sem, *index):
        return (sem.at[(0, *index)], sem.at[(1, *index)])

    barrier = pltpu.get_barrier_semaphore()

    def greet(device):
        pl.semaphore_signal(barrier, inc=1, device_id=device, device_id_type=MESH)

    for r in range(1, GROUP):
        greet(at_head(ahead[r]))
    for r in range(1, MATES):
        greet(at_mate((mate + r) % MATES))
    greet(sibling)

    row = iota((ROWS, ROWS), 0)
    col = iota((ROWS, ROWS), 1)
    split = one_hot(col == jnp.where(row < HALF, 2 * row, 2 * row - (ROWS - 1)))
    low = iota((ROWS, PAIR), 1) < HEAD_DIM

    for load in loads:
        load.wait()
    order = [[None, None] for _ in range(HEADS)]
    for which, (x_ref, y_ref, packed) in enumerate(
        ((k_ref, v_ref, send_kv), (q_ref, g_ref, send_qg))
    ):
        x_all = dot(split, x_ref[...])
        y_all = dot(split, y_ref[...])
        for t in range(HEADS // 2):
            x = x_all[:, t * PAIR : (t + 1) * PAIR]
            y = y_all[:, t * PAIR : (t + 1) * PAIR]
            for h, both in (
                (2 * t, jnp.where(low, x, pltpu.roll(y, HEAD_DIM, 1))),
                (2 * t + 1, jnp.where(low, pltpu.roll(x, HEAD_DIM, 1), y)),
            ):
                even = off_ref[1, h] == 0
                first = jnp.where(even, both[:HALF], both[HALF:]).astype(BF16)
                second = jnp.where(even, both[HALF:], both[:HALF]).astype(BF16)
                packed[h, 0] = first
                packed[h, 1] = second
                order[h][which] = [first, second]
    tile_row = iota((TILE, 2 * ROWS), 0)
    tile_col = iota((TILE, 2 * ROWS), 1)
    wanted = (tile_row >> 2) * ROWS + (tile_row & 3) * 16
    for h in range(HEADS):
        place = ((off_ref[1, h] + off_ref[2, h]) % 2) * HALF + (off_ref[2, h] >> 1)
        hit = one_hot((tile_col == wanted + place) & (tile_row < 8))
        send_few[h] = dot(hit, jnp.concatenate(order[h][0] + order[h][1], axis=0)).astype(BF16)

    pl.semaphore_wait(barrier, GROUP - 1 + MATES - 1 + 1)

    in_few, in_kv, in_qg = [], [], [[], []]
    for r in range(1, GROUP):
        other = ahead[r]
        tile = pl.ds(r * TILE, TILE)
        in_few.append(
            remote(send_few.at[other], few.at[tile, :], pair_of(few_sem, r), at_head(other))
        )
        in_few[-1].start()
    for r in range(1, GROUP):
        other = ahead[r]
        slot = pl.ds(r * HALF, HALF)
        in_kv.append(
            remote(send_kv.at[other], kv.at[:, slot, :], pair_of(kv_sem, r), at_head(other))
        )
        in_kv[-1].start()
    for half in range(2):
        for r in range(1, GROUP):
            other = ahead[r]
            slot = pl.ds(r * HALF, HALF)
            in_qg[half].append(
                remote(
                    send_qg.at[other, half],
                    qg.at[half, slot, :],
                    pair_of(qg_sem, half, r),
                    at_head(other),
                )
            )
            in_qg[half][-1].start()
    few[:TILE] = send_few[head]
    kv[:, :HALF] = send_kv[head]
    qg[:, :HALF] = send_qg[head]

    off1 = off_ref[1, head]
    off2 = off_ref[2, head]
    inside = (off1 + off2) % 2 == 0
    base = jnp.where(inside, 0, WIDE) + (off2 >> 1)
    at = iota((FEW, KEYS), 0)
    pick = iota((FEW, KEYS), 1) == base + (at >> 2) * HALF + (at & 3) * 16
    at = iota((KEYS, FEW), 1)
    pick_t = one_hot(iota((KEYS, FEW), 0) == base + (at >> 2) * HALF + (at & 3) * 16)
    pick_low = one_hot(pick)
    at = iota((2 * FEW, GROUP * TILE), 0)
    gather = one_hot(
        iota((2 * FEW, GROUP * TILE), 1)
        == ((at % FEW) >> 2) * TILE + (at & 3) + jnp.where(at < FEW, 0, 4)
    )
    for copy in in_few:
        copy.wait_recv()
    picked = dot(gather, few[...])
    keys2[0, mate] = picked[:FEW].astype(BF16)
    qg2 = picked[FEW:]

    def level2(r):
        block = keys2.at[0, mate]
        return remote(block, block, pair_of(l2_sem, r), at_mate((mate + r) % MATES))

    def level2_start(r, carry):
        level2(r).start()
        return carry

    lax.fori_loop(1, MATES, level2_start, 0)

    level1 = []
    for r in range(GROUP):
        if r:
            in_kv[r - 1].wait_recv()
        slot = pl.ds(r * HALF, HALF)
        level1.append(remote(kv.at[0, slot, :], peer.at[slot, :], pair_of(l1_sem, r), partner))
        level1[-1].start()

    lane_low = iota((1, PAIR), 1) < HEAD_DIM
    zero = jnp.zeros((), BF16)
    kv_all = kv[...].reshape(KEYS, PAIR)
    kv_k[:KEYS] = jnp.where(lane_low, kv_all, zero)
    kv_v[:KEYS] = jnp.where(lane_low, zero, kv_all)
    k_t[:, :KEYS] = kv_all.T[:HEAD_DIM]

    def level2_wait(r, carry):
        level2(r).wait_recv()
        return carry

    lax.fori_loop(1, MATES, level2_wait, 0)
    passed = remote(keys2.at[0], keys2.at[1], pair_of(pass_sem), sibling)
    passed.start()

    for copy in level1:
        copy.wait_recv()
    peer_all = peer[...]
    kv_k[KEYS:] = jnp.where(lane_low, peer_all, zero)
    kv_v[KEYS:] = jnp.where(lane_low, zero, peer_all)
    k_t[:, KEYS:] = peer_all.T[:HEAD_DIM]
    passed.wait_recv()

    few_low = iota((FEW, PAIR), 1) < HEAD_DIM
    q2 = jnp.where(few_low, qg2, 0.0).astype(BF16)
    g2 = jnp.where(few_low, 0.0, qg2).astype(BF16)
    both2 = jnp.concatenate([q2, g2], axis=0)
    kv2 = keys2[...].reshape(KEYS, PAIR)
    here = dot_nt(both2, kv_all)
    near = dot_nt(both2, peer_all)
    far = dot_nt(both2, kv2)
    s_here = here[:FEW] * TO_EXP2
    s_near = jnp.where(inside, near[:FEW] * TO_EXP2, LOWEST)
    s_far = far[:FEW] * TO_EXP2
    high2 = jnp.maximum(
        jnp.maximum(
            jnp.max(s_here, axis=1, keepdims=True), jnp.max(s_near, axis=1, keepdims=True)
        ),
        jnp.max(s_far, axis=1, keepdims=True),
    )
    twice = jnp.where((iota((FEW, KEYS), 1) < WIDE) & inside, 2.0, 1.0)
    e_here = jnp.exp2(s_here - high2) * twice
    e_near = jnp.exp2(s_near - high2)
    e_far = jnp.exp2(s_far - high2)
    sum2 = jnp.sum(e_far, axis=1, keepdims=True)
    dot2 = jnp.sum(e_far * far[FEW:], axis=1, keepdims=True)
    sum2_all = (
        sum2 + jnp.sum(e_here, axis=1, keepdims=True) + jnp.sum(e_near, axis=1, keepdims=True)
    )
    dot2_all = (
        dot2
        + jnp.sum(e_here * here[FEW:], axis=1, keepdims=True)
        + jnp.sum(e_near * near[FEW:], axis=1, keepdims=True)
    )
    inverse2 = 1.0 / sum2_all
    p2 = e_far * inverse2
    ds2 = p2 * (far[FEW:] - dot2_all * inverse2)
    scaled_q2 = (q2 * jnp.asarray(SCALE, BF16)).astype(BF16)
    kv_grad2 = dot(ds2.T.astype(BF16), scaled_q2) + dot(p2.T.astype(BF16), g2)
    part2[...] = kv_grad2[WIDE:].astype(BF16)
    halved = remote(part2, sib, pair_of(half_sem), sibling)
    halved.start()
    part2_own[...] = kv_grad2[:WIDE]
    dq2_parts = two_parts(dot(ds2.astype(BF16), kv2).T[:HEAD_DIM])
    high2_row = jnp.max(jnp.where(pick, high2, LOWEST), axis=0, keepdims=True)
    sum2_row = jnp.sum(jnp.where(pick, sum2, 0.0), axis=0, keepdims=True)
    dot2_row = jnp.sum(jnp.where(pick, dot2, 0.0), axis=0, keepdims=True)

    out_copies = []

    def block(c):
        half = c // 2
        first = (c % 2) * COLS
        columns = slice(c * COLS, (c + 1) * COLS)
        for r in range(max(1, first // HALF), first // HALF + SLOTS):
            in_qg[half][r - 1].wait_recv()
        mine = qg[half, first : first + COLS, :]
        across = mine.T
        scaled_q = jnp.where(lane_low, mine * jnp.asarray(SCALE, BF16), zero)
        only_g = jnp.where(lane_low, zero, mine)
        depth = KEYS + WIDE if half == 0 else KEYS
        steps = range(0, depth, DEEP)
        high8 = jnp.full((8, COLS), LOWEST, F32)
        for j in steps:
            s = dot(kv_k[j : j + DEEP], across) * TO_EXP2
            score[j : j + DEEP] = s
            high8 = jnp.maximum(high8, fold8(s, jnp.maximum))
        high = jnp.maximum(jnp.max(high8, axis=0, keepdims=True), high2_row[:, columns])
        sum8 = jnp.zeros((8, COLS), F32)
        dot8 = jnp.zeros((8, COLS), F32)

        def weight(j):
            return 2.0 if half == 0 and j < WIDE else 1.0

        for j in steps:
            e = jnp.exp2(score[j : j + DEEP] - high)
            score[j : j + DEEP] = e
            d = dot(kv_v[j : j + DEEP], across)
            dprob[j : j + DEEP] = d
            sum8 = sum8 + weight(j) * fold8(e, jnp.add)
            dot8 = dot8 + weight(j) * fold8(e * d, jnp.add)
        shift2 = jnp.exp2(high2_row[:, columns] - high)
        total = jnp.sum(sum8, axis=0, keepdims=True) + shift2 * sum2_row[:, columns]
        product = jnp.sum(dot8, axis=0, keepdims=True) + shift2 * dot2_row[:, columns]
        inverse = 1.0 / total
        delta = product * inverse
        for j in steps:
            p = score[j : j + DEEP] * (weight(j) * inverse)
            ds = (p * (dprob[j : j + DEEP] - delta)).astype(BF16)
            dsc[j : j + DEEP] = ds
            added = dot(ds, scaled_q) + dot(p.astype(BF16), only_g)
            acc[j : j + DEEP] = added if c == 0 else acc[j : j + DEEP] + added
        dq_t = dot(k_t[:, :depth], dsc[:depth])
        for part in dq2_parts:
            dq_t = dq_t + dot(part, pick_low[:, columns])
        dq = (dq_t * SCALE).T
        lanes = [
            jnp.concatenate([dq[i * HALF + b : i * HALF + b + QUARTER] for i in range(SLOTS)], 0)
            for b in (0, QUARTER)
        ]
        rows = slice((c % 2) * SLOTS * QUARTER, (c % 2 + 1) * SLOTS * QUARTER)
        out_q[half, rows] = jnp.concatenate(lanes, axis=1).astype(BF16)
        for r in range(first // HALF, first // HALF + SLOTS):
            slot = pl.ds(r * QUARTER, QUARTER)
            if r == 0:
                fin_q[half, head] = out_q[half, :QUARTER]
            else:
                copy = remote(
                    out_q.at[half, slot, :],
                    fin_q.at[half, head],
                    pair_of(dq_sem, half, r),
                    at_head(behind[r]),
                )
                copy.start()
                out_copies.append(copy)

    block(0)
    halved.wait_recv()
    back2[...] = (part2_own[...] + sib[...].astype(F32)).astype(BF16)

    def level2_back(r):
        other = (mate + r) % MATES
        return remote(
            back2.at[pl.ds(pl.multiple_of(other * FEW, FEW), FEW), :],
            got2.at[r],
            pair_of(b2_sem, r),
            at_mate(other),
        )

    def level2_back_start(r, carry):
        level2_back(r).start()
        return carry

    lax.fori_loop(1, MATES, level2_back_start, 0)
    block(1)
    part1[...] = acc[KEYS:].astype(BF16)
    back1 = remote(part1, got1, pair_of(b1_sem), partner)
    back1.start()
    block(2)
    block(3)

    def level2_back_wait(r, total):
        level2_back(r).wait_recv()
        return total + got2[r].astype(F32)

    own2 = back2[pl.ds(pl.multiple_of(mate * FEW, FEW), FEW), :].astype(F32)
    sum_few = lax.fori_loop(1, MATES, level2_back_wait, own2)
    upper, lower = two_parts(sum_few)
    added = dot(pick_t, upper) + dot(pick_t, lower)

    def go_home(half):
        for r in range(GROUP):
            slot = pl.ds(r * HALF, HALF)
            if r == 0:
                fin_kv[half, head] = out_kv[half, :HALF]
            else:
                copy = remote(
                    out_kv.at[half, slot, :],
                    fin_kv.at[half, head],
                    pair_of(home_sem, half, r),
                    at_head(behind[r]),
                )
                copy.start()
                out_copies.append(copy)

    out_kv[1] = (acc[WIDE:KEYS] + added[WIDE:]).astype(BF16)
    go_home(1)
    back1.wait_recv()
    out_kv[0] = (acc[:WIDE] + added[:WIDE] + got1[...].astype(F32)).astype(BF16)
    go_home(0)

    for copy in in_few + in_kv + in_qg[0] + in_qg[1] + level1 + [passed, halved, back1]:
        copy.wait_send()

    def sent2(r, carry):
        level2(r).wait_send()
        level2_back(r).wait_send()
        return carry

    lax.fori_loop(1, MATES, sent2, 0)

    for copy in out_copies:
        copy.wait()

    merge = one_hot(row == jnp.where(col < HALF, 2 * col, 2 * col - (ROWS - 1)))
    quarter_low = iota((QUARTER, PAIR), 1) < HEAD_DIM

    def ordered(ref, h):
        even = off_ref[1, h] == 0
        first = ref[0, h].astype(F32)
        second = ref[1, h].astype(F32)
        return jnp.where(even, first, second), jnp.where(even, second, first)

    for t in range(HEADS // 2):
        lanes = slice(t * PAIR, (t + 1) * PAIR)
        a = jnp.concatenate(ordered(fin_kv, 2 * t), axis=0)
        b = jnp.concatenate(ordered(fin_kv, 2 * t + 1), axis=0)
        dk = jnp.where(low, a, pltpu.roll(b, HEAD_DIM, 1)).astype(BF16)
        dv = jnp.where(low, pltpu.roll(a, HEAD_DIM, 1), b).astype(BF16)
        out_ref[1, :, lanes] = dot(merge, dk).astype(BF16)
        out_ref[2, :, lanes] = dot(merge, dv).astype(BF16)
        parts = []
        for a, b in zip(ordered(fin_q, 2 * t), ordered(fin_q, 2 * t + 1)):
            parts.append(jnp.where(quarter_low, a, pltpu.roll(b, HEAD_DIM, 1)))
            parts.append(jnp.where(quarter_low, pltpu.roll(a, HEAD_DIM, 1), b))
        dq = jnp.concatenate(parts, axis=0).astype(BF16)
        out_ref[0, :, lanes] = dot(merge, dq).astype(BF16)


def local(queries, keys, values, grad_out, offsets):
    width = HEADS * HEAD_DIM
    dma = pltpu.SemaphoreType.DMA

    def low_buffer(*shape):
        return pltpu.VMEM(shape, BF16)

    result = pl.pallas_call(
        kernel,
        out_shape=jax.ShapeDtypeStruct((3, ROWS, width), BF16),
        in_specs=[pl.BlockSpec(memory_space=pltpu.HBM)] * 5,
        out_specs=pl.BlockSpec(memory_space=pltpu.VMEM),
        scratch_shapes=[
            pltpu.SMEM((LEVELS, HEADS), jnp.int32),
            low_buffer(ROWS, width),
            low_buffer(ROWS, width),
            low_buffer(ROWS, width),
            low_buffer(ROWS, width),
            low_buffer(HEADS, TILE, PAIR),
            low_buffer(HEADS, 2, HALF, PAIR),
            low_buffer(HEADS, 2, HALF, PAIR),
            low_buffer(GROUP * TILE, PAIR),
            low_buffer(2, WIDE, PAIR),
            low_buffer(2, WIDE, PAIR),
            low_buffer(WIDE, PAIR),
            low_buffer(2, MATES, FEW, PAIR),
            low_buffer(KEYS + WIDE, PAIR),
            low_buffer(KEYS + WIDE, PAIR),
            low_buffer(HEAD_DIM, KEYS + WIDE),
            low_buffer(WIDE, PAIR),
            low_buffer(WIDE, PAIR),
            low_buffer(WIDE, PAIR),
            pltpu.VMEM((WIDE, PAIR), F32),
            low_buffer(WIDE, PAIR),
            low_buffer(WIDE, PAIR),
            low_buffer(MATES, FEW, PAIR),
            low_buffer(2, WIDE, PAIR),
            low_buffer(2, GROUP * QUARTER, PAIR),
            low_buffer(2, HEADS, HALF, PAIR),
            low_buffer(2, HEADS, QUARTER, PAIR),
            pltpu.VMEM((KEYS + WIDE, COLS), F32),
            pltpu.VMEM((KEYS + WIDE, COLS), F32),
            low_buffer(KEYS + WIDE, COLS),
            pltpu.VMEM((KEYS + WIDE, PAIR), F32),
            dma((2, GROUP)),
            dma((2, GROUP)),
            dma((2, 2, GROUP)),
            dma((2, GROUP)),
            dma((2, MATES)),
            dma((2,)),
            dma((2,)),
            dma((2,)),
            dma((2, MATES)),
            dma((2, 2, GROUP)),
            dma((2, 2, GROUP)),
            dma((5,)),
        ],
        compiler_params=pltpu.CompilerParams(
            collective_id=0, has_side_effects=True, vmem_limit_bytes=63 * 1024 * 1024
        ),
    )(offsets, queries, keys, values, grad_out)
    return result[0], result[1], result[2]


def solution(mesh):
    rows = P(("ctxa", "ctxb"), None)
    return jax.shard_map(
        local,
        mesh=mesh,
        in_specs=(rows, rows, rows, rows, P()),
        out_specs=(rows, rows, rows),
        check_vma=False,
    )
```

profile of v0, /device:TPU:1, one launch (start us, length us, event | category | flops | bytes accessed | tf_op | source)
XLA Modules:
  0.0 45.6 jit_solution(6506156113441443291)
XLA Ops:
  0.6 43.2 %shard_map.76 = bf16[3,128,512]{2,1,0:T(8,128)(2,1)} custom-call(s32[3,8]{1,0:T(4,128)} %off_hbm.1, bf16[128,512]{1,0:T(8,128)(2,1)} %q_hbm.1, bf16[128,512]{1,0:T(8,128)(2,1)} %k_hbm.1, bf16[128,512]{1,0:T(8,128)(2,1)} %v_hbm.1, bf16[128,512]{1,0:T(8,128)(2,1)} %g_hbm.1), custom_call_target="tpu_custom_call" | custom-call | tf_op jit(solution)/shard_map/pallas_call | solution.py:508
  43.8 1.8 %slice_bitcast_fusion = (bf16[128,512]{1,0:T(8,128)(2,1)}, bf16[128,512]{1,0:T(8,128)(2,1)}, bf16[128,512]{1,0:T(8,128)(2,1)}) fusion(bf16[3,128,512]{2,1,0:T(8,128)(2,1)} %shard_map.76), kind=kLoop, calls=%fused_computation | loop fusion | bytes 786432 | tf_op jit(solution)/shard_map/squeeze | solution.py:562
where the time goes:
time: 46.3 us; the launch traced here: 45.6 us
  Pallas kernels  43.2 us (93%)
  local copies, waits for them, and re-layouts  1.78 us (4%)
  between operations  0.64 us (1%)
    pallas_call x1, Pallas kernels, local(): pl.pallas_call(kernel, out_shape=jax.ShapeDtypeStruct((3, ROWS, width), B...  43.2 us
    squeeze x1, local copies, waits for them, and re-layouts, local(): return (result[0], result[1], result[2])  1.78 us

commit v1 on v0

v1 whole, which is shorter than its diff:
```python
import math

import jax
import jax.numpy as jnp
from jax import lax
from jax.experimental import pallas as pl
from jax.experimental.pallas import tpu as pltpu
from jax.sharding import PartitionSpec as P

HEADS = 8
HEAD_DIM = 64
KEYS = 1024
LEVELS = 3
ROWS = 128
HALF = ROWS // 2
GROUP = 8
MATES = 16
WIDE = 512
FEW = 32
TILE = 16
QUARTER = HALF // 2
PAIR = 2 * HEAD_DIM
SCALE = HEAD_DIM ** (-0.5)
TO_EXP2 = SCALE * math.log2(math.e)
LOWEST = -1e30
MESH = pl.DeviceIdType.MESH
F32 = jnp.float32
BF16 = jnp.bfloat16
COLS = 256
SLOTS = COLS // HALF
DEEP = 128
FAR_FIRST = (6, 2, 5, 7, 4, 1, 3)
LAYERS = 8
LAYERS_FAR_FIRST = (4, 3, 5, 2, 6, 1, 7)
MATES_FAR_FIRST = (9, 8, 7, 10, 6, 11, 5, 12, 4, 13, 3, 14, 2, 15, 1)


def dot(x, y):
    return jnp.dot(x, y, preferred_element_type=F32)


def dot_nt(x, y):
    return lax.dot_general(x, y, (((1,), (1,)), ((), ())), preferred_element_type=F32)


def iota(shape, dim):
    return lax.broadcasted_iota(jnp.int32, shape, dim)


def one_hot(hit):
    return hit.astype(F32).astype(BF16)


def two_parts(x):
    high = x.astype(BF16)
    return high, (x - high.astype(F32)).astype(BF16)


def fold8(x, op):
    parts = [x[8 * i : 8 * i + 8] for i in range(x.shape[0] // 8)]
    while len(parts) > 1:
        parts = [op(parts[i], parts[i + 1]) for i in range(0, len(parts), 2)]
    return parts[0]


def kernel(
    off_hbm,
    q_hbm,
    k_hbm,
    v_hbm,
    g_hbm,
    out_ref,
    off_ref,
    q_ref,
    k_ref,
    v_ref,
    g_ref,
    send_few,
    send_kv,
    send_qg,
    few,
    few1,
    kv,
    qg,
    peer,
    keys2,
    rows2,
    stats2,
    kv_k,
    kv_v,
    k_t,
    out_kv,
    out_q,
    out_l1,
    out_few,
    fin_kv,
    fin_q,
    fin_l1,
    fin_few,
    score,
    dprob,
    dsc,
    acc,
    base_kv,
    few_sem,
    kv_sem,
    qg_sem,
    l1_sem,
    l2_sem,
    pass_sem,
    dq_sem,
    home_sem,
    home1_sem,
    home2_sem,
    load_sem,
):
    major = lax.axis_index("ctxa")
    minor = lax.axis_index("ctxb")
    head = minor % GROUP
    mate = (major // 2) * 4 + minor // GROUP

    def member(dx, dy):
        x = (head % 4 + dx) % 4
        y = (head // 4 + dy) % 2
        return y * 4 + x

    def at_head(other):
        return (major, (minor // GROUP) * GROUP + other)

    def at_mate(other):
        return ((other // 4) * 2 + major % 2, (other % 4) * GROUP + head)

    layer = mate // 2

    def at_layer(other):
        return ((other // 2) * 2 + major % 2, (other % 2) * (2 * GROUP) + minor % (2 * GROUP))

    ahead = [member(r % 4, r // 4) for r in range(GROUP)]
    behind = [member(4 - r % 4, r // 4) for r in range(GROUP)]
    sibling = (major + 1 - 2 * (major % 2), minor)
    paired = minor // GROUP + 1 - 2 * ((minor // GROUP) % 2)

    def at_paired(other):
        return (major, paired * GROUP + other)

    def remote(src, dst, sems, device):
        return pltpu.make_async_remote_copy(
            src_ref=src,
            dst_ref=dst,
            send_sem=sems[0],
            recv_sem=sems[1],
            device_id=device,
            device_id_type=MESH,
        )

    def pair_of(sem, *index):
        return (sem.at[(0, *index)], sem.at[(1, *index)])

    barrier = pltpu.get_barrier_semaphore()

    def greet(device):
        pl.semaphore_signal(barrier, inc=1, device_id=device, device_id_type=MESH)

    for r in MATES_FAR_FIRST:
        greet(at_mate((mate + r) % MATES))
    for r in FAR_FIRST:
        greet(at_paired(behind[r]))
    for r in FAR_FIRST:
        greet(at_head(ahead[r]))
    greet(sibling)
    loads = []
    for i, (src, dst) in enumerate(
        ((k_hbm, k_ref), (v_hbm, v_ref), (q_hbm, q_ref), (g_hbm, g_ref), (off_hbm, off_ref))
    ):
        load = pltpu.make_async_copy(src, dst, load_sem.at[i])
        load.start()
        loads.append(load)

    row = iota((ROWS, ROWS), 0)
    col = iota((ROWS, ROWS), 1)
    split = one_hot(col == jnp.where(row < HALF, 2 * row, 2 * row - (ROWS - 1)))
    low = iota((ROWS, PAIR), 1) < HEAD_DIM

    for load in loads:
        load.wait()
    order = [[None, None] for _ in range(HEADS)]
    for which, (x_ref, y_ref, packed) in enumerate(
        ((k_ref, v_ref, send_kv), (q_ref, g_ref, send_qg))
    ):
        x_all = dot(split, x_ref[...])
        y_all = dot(split, y_ref[...])
        for t in range(HEADS // 2):
            x = x_all[:, t * PAIR : (t + 1) * PAIR]
            y = y_all[:, t * PAIR : (t + 1) * PAIR]
            for h, both in (
                (2 * t, jnp.where(low, x, pltpu.roll(y, HEAD_DIM, 1))),
                (2 * t + 1, jnp.where(low, pltpu.roll(x, HEAD_DIM, 1), y)),
            ):
                even = off_ref[1, h] == 0
                first = jnp.where(even, both[:HALF], both[HALF:]).astype(BF16)
                second = jnp.where(even, both[HALF:], both[:HALF]).astype(BF16)
                packed[h, 0] = first
                packed[h, 1] = second
                order[h][which] = [first, second]
    tile_row = iota((TILE, 2 * ROWS), 0)
    tile_col = iota((TILE, 2 * ROWS), 1)
    wanted = (tile_row >> 2) * ROWS + (tile_row & 3) * 16
    for h in range(HEADS):
        place = ((off_ref[1, h] + off_ref[2, h]) % 2) * HALF + (off_ref[2, h] >> 1)
        hit = one_hot((tile_col == wanted + place) & (tile_row < 8))
        send_few[h] = dot(hit, jnp.concatenate(order[h][0] + order[h][1], axis=0)).astype(BF16)

    pl.semaphore_wait(barrier, 2 * (GROUP - 1) + MATES - 1 + 1)

    in_few, in_few1, in_kv, in_l1, in_qg = {}, {}, {}, {}, [{}, {}]
    for r in FAR_FIRST:
        few_dst = few.at[pl.ds(r * TILE, TILE), :]
        in_few[r] = remote(send_few.at[ahead[r]], few_dst, pair_of(few_sem, 0, r), at_head(ahead[r]))
    for r in (*FAR_FIRST, 0):
        few_dst = few1.at[pl.ds(r * TILE, TILE), :]
        in_few1[r] = remote(
            send_few.at[ahead[r]], few_dst, pair_of(few_sem, 1, r), at_paired(ahead[r])
        )
    for r in FAR_FIRST:
        kv_dst = kv.at[:, pl.ds(r * HALF, HALF), :]
        in_kv[r] = remote(send_kv.at[ahead[r]], kv_dst, pair_of(kv_sem, r), at_head(ahead[r]))
        for half in range(2):
            qg_dst = qg.at[half, pl.ds(r * HALF, HALF), :]
            in_qg[half][r] = remote(
                send_qg.at[ahead[r], half], qg_dst, pair_of(qg_sem, half, r), at_head(ahead[r])
            )
    for r in (*FAR_FIRST, 0):
        l1_dst = peer.at[pl.ds(r * HALF, HALF), :]
        in_l1[r] = remote(
            send_kv.at[ahead[r], 0], l1_dst, pair_of(l1_sem, r), at_paired(ahead[r])
        )
    inward = (in_few, in_few1, in_kv, in_qg[1], in_l1, in_qg[0])
    for copies in inward:
        for copy in copies.values():
            copy.start()
    few[:TILE] = send_few[head]
    kv[:, :HALF] = send_kv[head]
    qg[:, :HALF] = send_qg[head]

    off1 = off_ref[1, head]
    off2 = off_ref[2, head]
    inside = (off1 + off2) % 2 == 0
    base = jnp.where(inside, 0, WIDE) + (off2 >> 1)
    at = iota((FEW, KEYS), 0)
    pick = iota((FEW, KEYS), 1) == base + (at >> 2) * HALF + (at & 3) * 16
    at = iota((KEYS, FEW), 1)
    pick_t = one_hot(iota((KEYS, FEW), 0) == base + (at >> 2) * HALF + (at & 3) * 16)
    pick_low = one_hot(pick)
    at = iota((2 * FEW, GROUP * TILE), 0)
    gather = one_hot(
        iota((2 * FEW, GROUP * TILE), 1)
        == ((at % FEW) >> 2) * TILE + (at & 3) + jnp.where(at < FEW, 0, 4)
    )
    for copy in (*in_few.values(), *in_few1.values()):
        copy.wait_recv()
    picked = dot(gather, few[...])
    picked1 = dot(gather, few1[...])
    own_kv2 = picked[:FEW]
    own_qg2 = picked[FEW:]
    mate1 = mate + 1 - 2 * (mate % 2)
    keys2[0, mate] = own_kv2.astype(BF16)
    rows2[0, mate] = own_qg2.astype(BF16)
    keys2[0, mate1] = picked1[:FEW].astype(BF16)
    rows2[0, mate1] = picked1[FEW:].astype(BF16)
    level2_refs = (keys2, rows2, stats2)

    layers = []
    for i in range(2):
        layers.append([])
        for r in LAYERS_FAR_FIRST:
            block = level2_refs[i].at[0, pl.ds(layer * 2, 2)]
            copy = remote(block, block, pair_of(l2_sem, i, r), at_layer((layer + r) % LAYERS))
            copy.start()
            layers[i].append(copy)

    def level2_pass(i):
        ref = level2_refs[i]
        copy = remote(ref.at[0], ref.at[1], pair_of(pass_sem, i), sibling)
        copy.start()
        return copy

    for copy in in_kv.values():
        copy.wait_recv()
    lane_low = iota((1, PAIR), 1) < HEAD_DIM
    zero = jnp.zeros((), BF16)
    kv_all = kv[...].reshape(KEYS, PAIR)
    kv_k[:KEYS] = jnp.where(lane_low, kv_all, zero)
    kv_v[:KEYS] = jnp.where(lane_low, zero, kv_all)
    k_t[:, :KEYS] = kv_all.T[:HEAD_DIM]

    def stats(c):
        half = c // 2
        first = (c % 2) * COLS
        for r in range(max(1, first // HALF), first // HALF + SLOTS):
            in_qg[half][r].wait_recv()
        across = qg[half, first : first + COLS, :].T
        steps = range(0, depth_of(c), DEEP)
        high8 = jnp.full((8, COLS), LOWEST, F32)
        for j in steps:
            s = dot(kv_k[j : j + DEEP], across) * TO_EXP2
            score[c, j : j + DEEP] = s
            high8 = jnp.maximum(high8, fold8(s, jnp.maximum))
        high = jnp.max(high8, axis=0, keepdims=True)
        sum8 = jnp.zeros((8, COLS), F32)
        dot8 = jnp.zeros((8, COLS), F32)
        for j in steps:
            e = jnp.exp2(score[c, j : j + DEEP] - high)
            score[c, j : j + DEEP] = e
            d = dot(kv_v[j : j + DEEP], across)
            dprob[c, j : j + DEEP] = d
            sum8 = sum8 + weight(c, j) * fold8(e, jnp.add)
            dot8 = dot8 + weight(c, j) * fold8(e * d, jnp.add)
        return (
            high,
            jnp.sum(sum8, axis=0, keepdims=True),
            jnp.sum(dot8, axis=0, keepdims=True),
        )

    def depth_of(c):
        return KEYS + WIDE if c < 2 else KEYS

    def weight(c, j):
        return 2.0 if c < 2 and j < WIDE else 1.0

    found = [None] * 4
    for c in (2, 3):
        found[c] = stats(c)
    for copy in in_l1.values():
        copy.wait_recv()
    peer_all = peer[...]
    kv_k[KEYS:] = jnp.where(lane_low, peer_all, zero)
    kv_v[KEYS:] = jnp.where(lane_low, zero, peer_all)
    k_t[:, KEYS:] = peer_all.T[:HEAD_DIM]
    for c in (0, 1):
        found[c] = stats(c)

    for copy in layers[0]:
        copy.wait_recv()
    passed_keys = level2_pass(0)
    passed_keys.wait_recv()

    few_low = iota((FEW, PAIR), 1) < HEAD_DIM
    both2 = jnp.concatenate(
        [jnp.where(few_low, own_qg2, 0.0), jnp.where(few_low, 0.0, own_qg2)], axis=0
    )
    kv2 = keys2[...].reshape(KEYS, PAIR)
    far = dot_nt(both2.astype(BF16), kv2)
    s2 = far[:FEW] * TO_EXP2
    d2 = far[FEW:]
    high2 = jnp.max(s2, axis=1, keepdims=True)
    e2 = jnp.exp2(s2 - high2)
    sum2 = jnp.sum(e2, axis=1, keepdims=True)
    dot2 = jnp.sum(e2 * d2, axis=1, keepdims=True)

    high, sums, products = [
        jnp.concatenate([found[c][i] for c in range(4)], axis=1) for i in range(3)
    ]
    high2_row = jnp.max(jnp.where(pick, high2, LOWEST), axis=0, keepdims=True)
    sum2_row = jnp.sum(jnp.where(pick, sum2, 0.0), axis=0, keepdims=True)
    dot2_row = jnp.sum(jnp.where(pick, dot2, 0.0), axis=0, keepdims=True)
    top = jnp.maximum(high, high2_row)
    factor = jnp.exp2(high - top)
    factor2 = jnp.exp2(high2_row - top)
    total = factor * sums + factor2 * sum2_row
    inverse = 1.0 / total
    delta = (factor * products + factor2 * dot2_row) * inverse
    factor = factor * inverse
    lse = top + jnp.log(total) * math.log2(math.e)
    lse2 = jnp.sum(jnp.where(pick, lse, 0.0), axis=1, keepdims=True)
    delta2 = jnp.sum(jnp.where(pick, delta, 0.0), axis=1, keepdims=True)

    lanes = iota((FEW, PAIR), 1) == (mate % 4) * FEW + iota((FEW, PAIR), 0)
    stats2[0, mate] = jnp.where(
        iota((8, PAIR), 0) == 0,
        jnp.sum(jnp.where(lanes, lse2, 0.0), axis=0, keepdims=True),
        jnp.sum(jnp.where(lanes, delta2, 0.0), axis=0, keepdims=True),
    )
    stat_block = stats2.at[0, mate]
    stat_copies = []
    for r in MATES_FAR_FIRST:
        copy = remote(stat_block, stat_block, pair_of(l2_sem, 2, r), at_mate((mate + r) % MATES))
        copy.start()
        stat_copies.append(copy)
    for copy in layers[1]:
        copy.wait_recv()
    passed_rows = level2_pass(1)
    ds2 = jnp.exp2(s2 - lse2) * (d2 - delta2)
    dq2_parts = two_parts(dot(ds2.astype(BF16), kv2).T[:HEAD_DIM])

    out_copies = []

    def grads(c, start):
        half = c // 2
        first = (c % 2) * COLS
        columns = slice(c * COLS, (c + 1) * COLS)
        mine = qg[half, first : first + COLS, :]
        scaled_q = jnp.where(lane_low, mine * jnp.asarray(SCALE, BF16), zero)
        only_g = jnp.where(lane_low, zero, mine)
        depth = depth_of(c)
        for j in range(0, depth, DEEP):
            p = score[c, j : j + DEEP] * (weight(c, j) * factor[:, columns])
            ds = (p * (dprob[c, j : j + DEEP] - delta[:, columns])).astype(BF16)
            dsc[j : j + DEEP] = ds
            added = dot(ds, scaled_q) + dot(p.astype(BF16), only_g)
            acc[j : j + DEEP] = added if start else acc[j : j + DEEP] + added
        dq_t = dot(k_t[:, :depth], dsc[:depth])
        for part in dq2_parts:
            dq_t = dq_t + dot(part, pick_low[:, columns])
        dq = (dq_t * SCALE).T
        sides = [
            jnp.concatenate([dq[i * HALF + b : i * HALF + b + QUARTER] for i in range(SLOTS)], 0)
            for b in (0, QUARTER)
        ]
        rows = slice((c % 2) * SLOTS * QUARTER, (c % 2 + 1) * SLOTS * QUARTER)
        out_q[half, rows] = jnp.concatenate(sides, axis=1).astype(BF16)
        for r in range(first // HALF, first // HALF + SLOTS):
            if r == 0:
                fin_q[half, head] = out_q[half, :QUARTER]
            else:
                copy = remote(
                    out_q.at[half, pl.ds(r * QUARTER, QUARTER), :],
                    fin_q.at[half, head],
                    pair_of(dq_sem, half, r),
                    at_head(behind[r]),
                )
                copy.start()
                out_copies.append(copy)

    grads(0, True)
    grads(1, False)
    out_l1[...] = acc[KEYS:].astype(BF16)
    for r in (*FAR_FIRST, 0):
        copy = remote(
            out_l1.at[pl.ds(r * HALF, HALF), :],
            fin_l1.at[head],
            pair_of(home1_sem, r),
            at_paired(behind[r]),
        )
        copy.start()
        out_copies.append(copy)
    grads(2, False)
    grads(3, False)
    out_kv[...] = acc[:KEYS].astype(BF16).reshape(2, WIDE, PAIR)
    fin_kv[head] = out_kv[:, :HALF]
    for r in FAR_FIRST:
        copy = remote(
            out_kv.at[:, pl.ds(r * HALF, HALF), :],
            fin_kv.at[head],
            pair_of(home_sem, r),
            at_head(behind[r]),
        )
        copy.start()
        out_copies.append(copy)

    passed_rows.wait_recv()
    qg2 = rows2[...].reshape(KEYS, PAIR)
    back = dot_nt(
        jnp.concatenate(
            [jnp.where(few_low, own_kv2, 0.0), jnp.where(few_low, 0.0, own_kv2)], axis=0
        ).astype(BF16),
        qg2,
    )
    for copy in stat_copies:
        copy.wait_recv()
    passed_stats = level2_pass(2)
    passed_stats.wait_recv()
    tiles = []
    for c in range(2):
        for m in range(0, MATES, 4):
            tiles.append(
                (stats2[c, m] + stats2[c, m + 1]) + (stats2[c, m + 2] + stats2[c, m + 3])
            )
    tiles = jnp.concatenate(tiles, axis=1)
    p2 = jnp.exp2(back[:FEW] * TO_EXP2 - tiles[0:1])
    ds2 = p2 * (back[FEW:] - tiles[1:2])
    scaled_q2 = jnp.where(lane_low, qg2 * jnp.asarray(SCALE, BF16), zero)
    only_g2 = jnp.where(lane_low, zero, qg2)
    kv_grad2 = dot(ds2.astype(BF16), scaled_q2) + dot(p2.astype(BF16), only_g2)
    at = iota((GROUP * TILE, FEW), 0)
    deal = one_hot(
        (iota((GROUP * TILE, FEW), 1) == (at >> 4) * 4 + (at & (TILE - 1)))
        & ((at & (TILE - 1)) < 4)
    )
    out_few[...] = dot(deal, kv_grad2.astype(BF16)).astype(BF16)
    fin_few[head] = out_few[:TILE]
    few_copies = []
    for r in FAR_FIRST:
        copy = remote(
            out_few.at[pl.ds(r * TILE, TILE), :],
            fin_few.at[head],
            pair_of(home2_sem, r),
            at_head(behind[r]),
        )
        copy.start()
        few_copies.append(copy)

    for copies in inward:
        for copy in copies.values():
            copy.wait_send()
    for copy in (*layers[0], *layers[1], *stat_copies, passed_keys, passed_rows, passed_stats):
        copy.wait_send()

    for copy in out_copies:
        copy.wait()

    merge = one_hot(row == jnp.where(col < HALF, 2 * col, 2 * col - (ROWS - 1)))
    quarter_low = iota((QUARTER, PAIR), 1) < HEAD_DIM

    def ordered(h, first, second):
        even = off_ref[1, h] == 0
        return jnp.where(even, first, second), jnp.where(even, second, first)

    def ordered_q(h):
        return ordered(h, fin_q[0, h].astype(F32), fin_q[1, h].astype(F32))

    def ordered_kv(h):
        first = fin_kv[h, 0].astype(F32) + fin_l1[h].astype(F32)
        return jnp.concatenate(ordered(h, first, fin_kv[h, 1].astype(F32)), axis=0)

    for t in range(HEADS // 2):
        lanes = slice(t * PAIR, (t + 1) * PAIR)
        a = ordered_kv(2 * t)
        b = ordered_kv(2 * t + 1)
        dk = jnp.where(low, a, pltpu.roll(b, HEAD_DIM, 1))
        dv = jnp.where(low, pltpu.roll(a, HEAD_DIM, 1), b)
        for i, x in enumerate((dk, dv)):
            upper, lower = two_parts(x)
            base_kv[i, :, lanes] = dot(merge, upper) + dot(merge, lower)
        parts = []
        for a, b in zip(ordered_q(2 * t), ordered_q(2 * t + 1)):
            parts.append(jnp.where(quarter_low, a, pltpu.roll(b, HEAD_DIM, 1)))
            parts.append(jnp.where(quarter_low, pltpu.roll(a, HEAD_DIM, 1), b))
        dq = jnp.concatenate(parts, axis=0).astype(BF16)
        out_ref[0, :, lanes] = dot(merge, dq).astype(BF16)
    tile_low = iota((TILE, PAIR), 1) < HEAD_DIM
    hits = []
    for h in range(HEADS):
        tile_row = iota((ROWS, TILE), 0)
        tile_col = iota((ROWS, TILE), 1)
        hits.append(((tile_row == off_ref[2, h] + tile_col * FEW) & (tile_col < 4)).astype(F32))
    hits = [jnp.concatenate(hits[i : i + 2], axis=1).astype(BF16) for i in range(0, HEADS, 2)]

    for copy in few_copies:
        copy.wait()
    for t in range(HEADS // 2):
        lanes = slice(t * PAIR, (t + 1) * PAIR)
        a = fin_few[2 * t].astype(F32)
        b = fin_few[2 * t + 1].astype(F32)
        dk = (jnp.where(tile_low, a, 0.0), jnp.where(tile_low, 0.0, pltpu.roll(b, HEAD_DIM, 1)))
        dv = (jnp.where(tile_low, pltpu.roll(a, HEAD_DIM, 1), 0.0), jnp.where(tile_low, 0.0, b))
        for i, x in enumerate((dk, dv)):
            added = dot(hits[t], jnp.concatenate(x, axis=0).astype(BF16))
            out_ref[i + 1, :, lanes] = (base_kv[i, :, lanes] + added).astype(BF16)


def local(queries, keys, values, grad_out, offsets):
    width = HEADS * HEAD_DIM
    dma = pltpu.SemaphoreType.DMA

    def low_buffer(*shape):
        return pltpu.VMEM(shape, BF16)

    result = pl.pallas_call(
        kernel,
        out_shape=jax.ShapeDtypeStruct((3, ROWS, width), BF16),
        in_specs=[pl.BlockSpec(memory_space=pltpu.HBM)] * 5,
        out_specs=pl.BlockSpec(memory_space=pltpu.VMEM),
        scratch_shapes=[
            pltpu.SMEM((LEVELS, HEADS), jnp.int32),
            low_buffer(ROWS, width),
            low_buffer(ROWS, width),
            low_buffer(ROWS, width),
            low_buffer(ROWS, width),
            low_buffer(HEADS, TILE, PAIR),
            low_buffer(HEADS, 2, HALF, PAIR),
            low_buffer(HEADS, 2, HALF, PAIR),
            low_buffer(GROUP * TILE, PAIR),
            low_buffer(GROUP * TILE, PAIR),
            low_buffer(2, WIDE, PAIR),
            low_buffer(2, WIDE, PAIR),
            low_buffer(WIDE, PAIR),
            low_buffer(2, MATES, FEW, PAIR),
            low_buffer(2, MATES, FEW, PAIR),
            pltpu.VMEM((2, MATES, 8, PAIR), F32),
            low_buffer(KEYS + WIDE, PAIR),
            low_buffer(KEYS + WIDE, PAIR),
            low_buffer(HEAD_DIM, KEYS + WIDE),
            low_buffer(2, WIDE, PAIR),
            low_buffer(2, GROUP * QUARTER, PAIR),
            low_buffer(WIDE, PAIR),
            low_buffer(GROUP * TILE, PAIR),
            low_buffer(HEADS, 2, HALF, PAIR),
            low_buffer(2, HEADS, QUARTER, PAIR),
            low_buffer(HEADS, HALF, PAIR),
            low_buffer(HEADS, TILE, PAIR),
            pltpu.VMEM((4, KEYS + WIDE, COLS), F32),
            pltpu.VMEM((4, KEYS + WIDE, COLS), F32),
            low_buffer(KEYS + WIDE, COLS),
            pltpu.VMEM((KEYS + WIDE, PAIR), F32),
            pltpu.VMEM((2, ROWS, width), F32),
            dma((2, 2, GROUP)),
            dma((2, GROUP)),
            dma((2, 2, GROUP)),
            dma((2, GROUP)),
            dma((2, 3, MATES)),
            dma((2, 3)),
            dma((2, 2, GROUP)),
            dma((2, GROUP)),
            dma((2, GROUP)),
            dma((2, GROUP)),
            dma((5,)),
        ],
        compiler_params=pltpu.CompilerParams(
            collective_id=0, has_side_effects=True, vmem_limit_bytes=63 * 1024 * 1024
        ),
    )(offsets, queries, keys, values, grad_out)
    return result[0], result[1], result[2]


def solution(mesh):
    rows = P(("ctxa", "ctxb"), None)
    return jax.shard_map(
        local,
        mesh=mesh,
        in_specs=(rows, rows, rows, rows, P()),
        out_specs=(rows, rows, rows),
        check_vma=False,
    )
```

time: 46.3 us -> 41.2 us (0.89); the launches traced: 45.6 us -> 41.1 us
  Pallas kernels: 43.2 us -> 38.7 us
    pallas_call x1, Pallas kernels: 43.2 us -> 38.7 us  [local(): pl.pallas_call(kernel, out_shape=jax.ShapeDtypeStruct((3, ROWS, width), B...]
where the time goes in v1:
time: 41.2 us; the launch traced here: 41.1 us
  Pallas kernels  38.7 us (94%)
  local copies, waits for them, and re-layouts  1.78 us (4%)
  between operations  0.64 us (2%)
    pallas_call x1, Pallas kernels, local(): pl.pallas_call(kernel, out_shape=jax.ShapeDtypeStruct((3, ROWS, width), B...  38.7 us
    squeeze x1, local copies, waits for them, and re-layouts, local(): return (result[0], result[1], result[2])  1.78 us

profile of v1, /device:TPU:1, one launch (start us, length us, event | category | flops | bytes accessed | tf_op | source)
XLA Modules:
  0.0 41.1 jit_solution(6882000069105241825)
XLA Ops:
  0.6 38.7 %shard_map.76 = bf16[3,128,512]{2,1,0:T(8,128)(2,1)} custom-call(s32[3,8]{1,0:T(4,128)} %off_hbm.1, bf16[128,512]{1,0:T(8,128)(2,1)} %q_hbm.1, bf16[128,512]{1,0:T(8,128)(2,1)} %k_hbm.1, bf16[128,512]{1,0:T(8,128)(2,1)} %v_hbm.1, bf16[128,512]{1,0:T(8,128)(2,1)} %g_hbm.1), custom_call_target="tpu_custom_call" | custom-call | tf_op jit(solution)/shard_map/pallas_call | solution.py:568
  39.3 1.8 %slice_bitcast_fusion = (bf16[128,512]{1,0:T(8,128)(2,1)}, bf16[128,512]{1,0:T(8,128)(2,1)}, bf16[128,512]{1,0:T(8,128)(2,1)}) fusion(bf16[3,128,512]{2,1,0:T(8,128)(2,1)} %shard_map.76), kind=kLoop, calls=%fused_computation | loop fusion | bytes 786432 | tf_op jit(solution)/shard_map/squeeze | solution.py:622

commit v2 on v1

--- a/solution.py
+++ b/solution.py
@@ -29,8 +29,24 @@
 COLS = 256
 SLOTS = COLS // HALF
 DEEP = 128
+KINDS = 18
+(
+    FEW_OWN,
+    FEW_PAIRED,
+    KV,
+    LEVEL1,
+    QG,
+    GATHER,
+    PASS,
+    STAT,
+    HOME_DQ,
+    HOME_KV,
+    HOME1,
+    HOME2,
+) = (0, 1, 2, 3, 4, 8, 10, 13, 14, 15, 16, 17)
 FAR_FIRST = (6, 2, 5, 7, 4, 1, 3)
 LAYERS = 8
+NEAR_LAYERS = (2, 6, 1, 7)
 LAYERS_FAR_FIRST = (4, 3, 5, 2, 6, 1, 7)
 MATES_FAR_FIRST = (9, 8, 7, 10, 6, 11, 5, 12, 4, 13, 3, 14, 2, 15, 1)
 
@@ -69,12 +85,9 @@
     k_hbm,
     v_hbm,
     g_hbm,
-    out_ref,
+    out_hbm,
     off_ref,
-    q_ref,
-    k_ref,
-    v_ref,
-    g_ref,
+    in_ref,
     send_few,
     send_kv,
     send_qg,
@@ -102,18 +115,20 @@
     dsc,
     acc,
     base_kv,
-    few_sem,
-    kv_sem,
-    qg_sem,
-    l1_sem,
-    l2_sem,
-    pass_sem,
-    dq_sem,
-    home_sem,
-    home1_sem,
-    home2_sem,
+    out_ref,
+    send_sem,
+    recv_sem,
     load_sem,
+    hop_sem,
 ):
+    loads = [
+        pltpu.make_async_copy(src, in_ref.at[i], load_sem.at[0])
+        for i, src in enumerate((k_hbm, v_hbm, q_hbm, g_hbm))
+    ]
+    loads.append(pltpu.make_async_copy(off_hbm, off_ref, load_sem.at[1]))
+    for load in loads:
+        load.start()
+
     major = lax.axis_index("ctxa")
     minor = lax.axis_index("ctxb")
     head = minor % GROUP
@@ -143,52 +158,45 @@
     def at_paired(other):
         return (major, paired * GROUP + other)
 
-    def remote(src, dst, sems, device):
-        return pltpu.make_async_remote_copy(
+    def send(src, dst, kind, device):
+        pltpu.make_async_remote_copy(
             src_ref=src,
             dst_ref=dst,
-            send_sem=sems[0],
-            recv_sem=sems[1],
+            send_sem=send_sem.at[kind],
+            recv_sem=recv_sem.at[kind],
             device_id=device,
             device_id_type=MESH,
-        )
-
-    def pair_of(sem, *index):
-        return (sem.at[(0, *index)], sem.at[(1, *index)])
+        ).start()
+
+    def received(kind, amount):
+        pltpu.make_async_copy(amount, amount, recv_sem.at[kind]).wait()
+
+    def sent(kind, amount):
+        pltpu.make_async_copy(amount, amount, send_sem.at[kind]).wait()
 
     barrier = pltpu.get_barrier_semaphore()
 
     def greet(device):
         pl.semaphore_signal(barrier, inc=1, device_id=device, device_id_type=MESH)
 
-    for r in MATES_FAR_FIRST:
-        greet(at_mate((mate + r) % MATES))
-    for r in FAR_FIRST:
-        greet(at_paired(behind[r]))
     for r in FAR_FIRST:
         greet(at_head(ahead[r]))
+    for r in (*FAR_FIRST, 0):
+        greet(at_paired(behind[r]))
+    for r in NEAR_LAYERS:
+        greet(at_layer((layer + r) % LAYERS))
     greet(sibling)
-    loads = []
-    for i, (src, dst) in enumerate(
-        ((k_hbm, k_ref), (v_hbm, v_ref), (q_hbm, q_ref), (g_hbm, g_ref), (off_hbm, off_ref))
-    ):
-        load = pltpu.make_async_copy(src, dst, load_sem.at[i])
-        load.start()
-        loads.append(load)
-
     row = iota((ROWS, ROWS), 0)
     col = iota((ROWS, ROWS), 1)
     split = one_hot(col == jnp.where(row < HALF, 2 * row, 2 * row - (ROWS - 1)))
     low = iota((ROWS, PAIR), 1) < HEAD_DIM
 
-    for load in loads:
-        load.wait()
+    pltpu.make_async_copy(in_ref, in_ref, load_sem.at[0]).wait()
+    loads[4].wait()
     order = [[None, None] for _ in range(HEADS)]
-    for which, (x_ref, y_ref, packed) in enumerate(
-        ((k_ref, v_ref, send_kv), (q_ref, g_ref, send_qg))
-    ):
-        x_all = dot(split, x_ref[...])
-        y_all = dot(split, y_ref[...])
+    for which, packed in enumerate((send_kv, send_qg)):
+        x_all = dot(split, in_ref[2 * which])
+        y_all = dot(split, in_ref[2 * which + 1])
         for t in range(HEADS // 2):
             x = x_all[:, t * PAIR : (t + 1) * PAIR]
             y = y_all[:, t * PAIR : (t + 1) * PAIR]
@@ -210,34 +218,33 @@
         hit = one_hot((tile_col == wanted + place) & (tile_row < 8))
         send_few[h] = dot(hit, jnp.concatenate(order[h][0] + order[h][1], axis=0)).astype(BF16)
 
-    pl.semaphore_wait(barrier, 2 * (GROUP - 1) + MATES - 1 + 1)
-
-    in_few, in_few1, in_kv, in_l1, in_qg = {}, {}, {}, {}, [{}, {}]
+    pl.semaphore_wait(barrier, GROUP - 1 + GROUP + len(NEAR_LAYERS) + 1)
+
     for r in FAR_FIRST:
-        few_dst = few.at[pl.ds(r * TILE, TILE), :]
-        in_few[r] = remote(send_few.at[ahead[r]], few_dst, pair_of(few_sem, 0, r), at_head(ahead[r]))
+        tile = few.at[pl.ds(r * TILE, TILE), :]
+        send(send_few.at[ahead[r]], tile, FEW_OWN, at_head(ahead[r]))
     for r in (*FAR_FIRST, 0):
-        few_dst = few1.at[pl.ds(r * TILE, TILE), :]
-        in_few1[r] = remote(
-            send_few.at[ahead[r]], few_dst, pair_of(few_sem, 1, r), at_paired(ahead[r])
+        tile = few1.at[pl.ds(r * TILE, TILE), :]
+        send(send_few.at[ahead[r]], tile, FEW_PAIRED, at_paired(ahead[r]))
+    for r in NEAR_LAYERS[:2]:
+        pl.semaphore_signal(
+            hop_sem, inc=1, device_id=at_layer((layer + r) % LAYERS), device_id_type=MESH
         )
     for r in FAR_FIRST:
-        kv_dst = kv.at[:, pl.ds(r * HALF, HALF), :]
-        in_kv[r] = remote(send_kv.at[ahead[r]], kv_dst, pair_of(kv_sem, r), at_head(ahead[r]))
-        for half in range(2):
-            qg_dst = qg.at[half, pl.ds(r * HALF, HALF), :]
-            in_qg[half][r] = remote(
-                send_qg.at[ahead[r], half], qg_dst, pair_of(qg_sem, half, r), at_head(ahead[r])
-            )
+        slot = kv.at[:, pl.ds(r * HALF, HALF), :]
+        send(send_kv.at[ahead[r]], slot, KV, at_head(ahead[r]))
     for r in (*FAR_FIRST, 0):
-        l1_dst = peer.at[pl.ds(r * HALF, HALF), :]
-        in_l1[r] = remote(
-            send_kv.at[ahead[r], 0], l1_dst, pair_of(l1_sem, r), at_paired(ahead[r])
-        )
-    inward = (in_few, in_few1, in_kv, in_qg[1], in_l1, in_qg[0])
-    for copies in inward:
-        for copy in copies.values():
-            copy.start()
+        slot = peer.at[pl.ds(r * HALF, HALF), :]
+        send(send_kv.at[ahead[r], 0], slot, LEVEL1, at_paired(ahead[r]))
+
+    def block_kind(c):
+        return QG + c
+
+    for half in (1, 0):
+        for r in FAR_FIRST:
+            slot = qg.at[half, pl.ds(r * HALF, HALF), :]
+            kind = block_kind(2 * half + r // SLOTS)
+            send(send_qg.at[ahead[r], half], slot, kind, at_head(ahead[r]))
     few[:TILE] = send_few[head]
     kv[:, :HALF] = send_kv[head]
     qg[:, :HALF] = send_qg[head]
@@ -256,8 +263,9 @@
         iota((2 * FEW, GROUP * TILE), 1)
         == ((at % FEW) >> 2) * TILE + (at & 3) + jnp.where(at < FEW, 0, 4)
     )
-    for copy in (*in_few.values(), *in_few1.values()):
-        copy.wait_recv()
+    pl.semaphore_wait(hop_sem, 2)
+    received(FEW_OWN, few.at[pl.ds(TILE, (GROUP - 1) * TILE)])
+    received(FEW_PAIRED, few1)
     picked = dot(gather, few[...])
     picked1 = dot(gather, few1[...])
     own_kv2 = picked[:FEW]
@@ -267,25 +275,13 @@
     rows2[0, mate] = own_qg2.astype(BF16)
     keys2[0, mate1] = picked1[:FEW].astype(BF16)
     rows2[0, mate1] = picked1[FEW:].astype(BF16)
-    level2_refs = (keys2, rows2, stats2)
-
-    layers = []
-    for i in range(2):
-        layers.append([])
+    for i, ref in enumerate((keys2, rows2)):
+        block = ref.at[0, pl.ds(layer * 2, 2)]
         for r in LAYERS_FAR_FIRST:
-            block = level2_refs[i].at[0, pl.ds(layer * 2, 2)]
-            copy = remote(block, block, pair_of(l2_sem, i, r), at_layer((layer + r) % LAYERS))
-            copy.start()
-            layers[i].append(copy)
-
-    def level2_pass(i):
-        ref = level2_refs[i]
-        copy = remote(ref.at[0], ref.at[1], pair_of(pass_sem, i), sibling)
-        copy.start()
-        return copy
-
-    for copy in in_kv.values():
-        copy.wait_recv()
+            send(block, block, GATHER + i, at_layer((layer + r) % LAYERS))
+    other_layers = keys2.at[0, pl.ds(0, MATES - 2)]
+
+    received(KV, kv.at[:, pl.ds(HALF, WIDE - HALF), :])
     lane_low = iota((1, PAIR), 1) < HEAD_DIM
     zero = jnp.zeros((), BF16)
     kv_all = kv[...].reshape(KEYS, PAIR)
@@ -293,11 +289,14 @@
     kv_v[:KEYS] = jnp.where(lane_low, zero, kv_all)
     k_t[:, :KEYS] = kv_all.T[:HEAD_DIM]
 
+    def block_slots(c):
+        slots = SLOTS if c % 2 else SLOTS - 1
+        return qg.at[c // 2, pl.ds(WIDE - COLS, slots * HALF), :]
+
     def stats(c):
         half = c // 2
         first = (c % 2) * COLS
-        for r in range(max(1, first // HALF), first // HALF + SLOTS):
-            in_qg[half][r].wait_recv()
+        received(block_kind(c), block_slots(c))
         across = qg[half, first : first + COLS, :].T
         steps = range(0, depth_of(c), DEEP)
         high8 = jnp.full((8, COLS), LOWEST, F32)
@@ -327,35 +326,66 @@
     def weight(c, j):
         return 2.0 if c < 2 and j < WIDE else 1.0
 
-    found = [None] * 4
-    for c in (2, 3):
-        found[c] = stats(c)
-    for copy in in_l1.values():
-        copy.wait_recv()
+    received(LEVEL1, peer)
     peer_all = peer[...]
     kv_k[KEYS:] = jnp.where(lane_low, peer_all, zero)
     kv_v[KEYS:] = jnp.where(lane_low, zero, peer_all)
     k_t[:, KEYS:] = peer_all.T[:HEAD_DIM]
-    for c in (0, 1):
+    found = [None] * 4
+    for c in (2, 3):
         found[c] = stats(c)
-
-    for copy in layers[0]:
-        copy.wait_recv()
-    passed_keys = level2_pass(0)
-    passed_keys.wait_recv()
+    received(GATHER, other_layers)
+    send(keys2.at[0], keys2.at[1], PASS, sibling)
+    found[0] = stats(0)
+    received(PASS, keys2.at[0])
 
     few_low = iota((FEW, PAIR), 1) < HEAD_DIM
     both2 = jnp.concatenate(
         [jnp.where(few_low, own_qg2, 0.0), jnp.where(few_low, 0.0, own_qg2)], axis=0
-    )
+    ).astype(BF16)
     kv2 = keys2[...].reshape(KEYS, PAIR)
-    far = dot_nt(both2.astype(BF16), kv2)
+    here = dot_nt(both2, kv_all)
+    near = dot_nt(both2, peer_all)
+    far = dot_nt(both2, kv2)
+    s_here = here[:FEW] * TO_EXP2
+    s_near = jnp.where(inside, near[:FEW] * TO_EXP2, LOWEST)
     s2 = far[:FEW] * TO_EXP2
     d2 = far[FEW:]
-    high2 = jnp.max(s2, axis=1, keepdims=True)
+    high2 = jnp.maximum(
+        jnp.maximum(
+            jnp.max(s_here, axis=1, keepdims=True), jnp.max(s_near, axis=1, keepdims=True)
+        ),
+        jnp.max(s2, axis=1, keepdims=True),
+    )
+    twice = jnp.where((iota((FEW, KEYS), 1) < WIDE) & inside, 2.0, 1.0)
+    e_here = jnp.exp2(s_here - high2) * twice
+    e_near = jnp.exp2(s_near - high2)
     e2 = jnp.exp2(s2 - high2)
     sum2 = jnp.sum(e2, axis=1, keepdims=True)
     dot2 = jnp.sum(e2 * d2, axis=1, keepdims=True)
+    total2 = sum2 + jnp.sum(e_here, axis=1, keepdims=True) + jnp.sum(e_near, axis=1, keepdims=True)
+    product2 = (
+        dot2
+        + jnp.sum(e_here * here[FEW:], axis=1, keepdims=True)
+        + jnp.sum(e_near * near[FEW:], axis=1, keepdims=True)
+    )
+    lse2 = high2 + jnp.log(total2) * math.log2(math.e)
+    delta2 = product2 / total2
+    lanes = iota((FEW, PAIR), 1) == (mate % 4) * FEW + iota((FEW, PAIR), 0)
+    stats2[0, mate] = jnp.where(
+        iota((8, PAIR), 0) == 0,
+        jnp.sum(jnp.where(lanes, lse2, 0.0), axis=0, keepdims=True),
+        jnp.sum(jnp.where(lanes, delta2, 0.0), axis=0, keepdims=True),
+    )
+    stat_block = stats2.at[0, mate]
+    for r in MATES_FAR_FIRST:
+        send(stat_block, stat_block, STAT, at_mate((mate + r) % MATES))
+    received(GATHER + 1, other_layers)
+    send(rows2.at[0], rows2.at[1], PASS + 1, sibling)
+    ds2 = jnp.exp2(s2 - lse2) * (d2 - delta2)
+    dq2_parts = two_parts(dot(ds2.astype(BF16), kv2).T[:HEAD_DIM])
+
+    found[1] = stats(1)
 
     high, sums, products = [
         jnp.concatenate([found[c][i] for c in range(4)], axis=1) for i in range(3)
@@ -366,33 +396,9 @@
     top = jnp.maximum(high, high2_row)
     factor = jnp.exp2(high - top)
     factor2 = jnp.exp2(high2_row - top)
-    total = factor * sums + factor2 * sum2_row
-    inverse = 1.0 / total
+    inverse = 1.0 / (factor * sums + factor2 * sum2_row)
     delta = (factor * products + factor2 * dot2_row) * inverse
     factor = factor * inverse
-    lse = top + jnp.log(total) * math.log2(math.e)
-    lse2 = jnp.sum(jnp.where(pick, lse, 0.0), axis=1, keepdims=True)
-    delta2 = jnp.sum(jnp.where(pick, delta, 0.0), axis=1, keepdims=True)
-
-    lanes = iota((FEW, PAIR), 1) == (mate % 4) * FEW + iota((FEW, PAIR), 0)
-    stats2[0, mate] = jnp.where(
-        iota((8, PAIR), 0) == 0,
-        jnp.sum(jnp.where(lanes, lse2, 0.0), axis=0, keepdims=True),
-        jnp.sum(jnp.where(lanes, delta2, 0.0), axis=0, keepdims=True),
-    )
-    stat_block = stats2.at[0, mate]
-    stat_copies = []
-    for r in MATES_FAR_FIRST:
-        copy = remote(stat_block, stat_block, pair_of(l2_sem, 2, r), at_mate((mate + r) % MATES))
-        copy.start()
-        stat_copies.append(copy)
-    for copy in layers[1]:
-        copy.wait_recv()
-    passed_rows = level2_pass(1)
-    ds2 = jnp.exp2(s2 - lse2) * (d2 - delta2)
-    dq2_parts = two_parts(dot(ds2.astype(BF16), kv2).T[:HEAD_DIM])
-
-    out_copies = []
 
     def grads(c, start):
         half = c // 2
@@ -422,42 +428,24 @@
             if r == 0:
                 fin_q[half, head] = out_q[half, :QUARTER]
             else:
-                copy = remote(
-                    out_q.at[half, pl.ds(r * QUARTER, QUARTER), :],
-                    fin_q.at[half, head],
-                    pair_of(dq_sem, half, r),
-                    at_head(behind[r]),
-                )
-                copy.start()
-                out_copies.append(copy)
+                slot = out_q.at[half, pl.ds(r * QUARTER, QUARTER), :]
+                send(slot, fin_q.at[half, head], HOME_DQ, at_head(behind[r]))
 
     grads(0, True)
     grads(1, False)
     out_l1[...] = acc[KEYS:].astype(BF16)
     for r in (*FAR_FIRST, 0):
-        copy = remote(
-            out_l1.at[pl.ds(r * HALF, HALF), :],
-            fin_l1.at[head],
-            pair_of(home1_sem, r),
-            at_paired(behind[r]),
-        )
-        copy.start()
-        out_copies.append(copy)
+        slot = out_l1.at[pl.ds(r * HALF, HALF), :]
+        send(slot, fin_l1.at[head], HOME1, at_paired(behind[r]))
     grads(2, False)
     grads(3, False)
     out_kv[...] = acc[:KEYS].astype(BF16).reshape(2, WIDE, PAIR)
     fin_kv[head] = out_kv[:, :HALF]
     for r in FAR_FIRST:
-        copy = remote(
-            out_kv.at[:, pl.ds(r * HALF, HALF), :],
-            fin_kv.at[head],
-            pair_of(home_sem, r),
-            at_head(behind[r]),
-        )
-        copy.start()
-        out_copies.append(copy)
-
-    passed_rows.wait_recv()
+        slot = out_kv.at[:, pl.ds(r * HALF, HALF), :]
+        send(slot, fin_kv.at[head], HOME_KV, at_head(behind[r]))
+
+    received(PASS + 1, rows2.at[0])
     qg2 = rows2[...].reshape(KEYS, PAIR)
     back = dot_nt(
         jnp.concatenate(
@@ -465,10 +453,10 @@
         ).astype(BF16),
         qg2,
     )
-    for copy in stat_copies:
-        copy.wait_recv()
-    passed_stats = level2_pass(2)
-    passed_stats.wait_recv()
+    other_mates = stats2.at[0, pl.ds(0, MATES - 1)]
+    received(STAT, other_mates)
+    send(stats2.at[0], stats2.at[1], PASS + 2, sibling)
+    received(PASS + 2, stats2.at[0])
     tiles = []
     for c in range(2):
         for m in range(0, MATES, 4):
@@ -488,25 +476,27 @@
     )
     out_few[...] = dot(deal, kv_grad2.astype(BF16)).astype(BF16)
     fin_few[head] = out_few[:TILE]
-    few_copies = []
     for r in FAR_FIRST:
-        copy = remote(
-            out_few.at[pl.ds(r * TILE, TILE), :],
-            fin_few.at[head],
-            pair_of(home2_sem, r),
-            at_head(behind[r]),
-        )
-        copy.start()
-        few_copies.append(copy)
-
-    for copies in inward:
-        for copy in copies.values():
-            copy.wait_send()
-    for copy in (*layers[0], *layers[1], *stat_copies, passed_keys, passed_rows, passed_stats):
-        copy.wait_send()
-
-    for copy in out_copies:
-        copy.wait()
+        send(out_few.at[pl.ds(r * TILE, TILE), :], fin_few.at[head], HOME2, at_head(behind[r]))
+
+    sent(FEW_OWN, few.at[pl.ds(TILE, (GROUP - 1) * TILE)])
+    sent(FEW_PAIRED, few1)
+    sent(KV, kv.at[:, pl.ds(HALF, WIDE - HALF), :])
+    sent(LEVEL1, peer)
+    for c in range(4):
+        sent(block_kind(c), block_slots(c))
+    sent(GATHER, other_layers)
+    sent(GATHER + 1, other_layers)
+    sent(PASS, keys2.at[0])
+    sent(PASS + 1, rows2.at[0])
+    sent(PASS + 2, stats2.at[0])
+    sent(STAT, other_mates)
+
+    others = pl.ds(0, HEADS - 1)
+    for done in (received, sent):
+        done(HOME_DQ, fin_q.at[:, others])
+        done(HOME1, fin_l1)
+        done(HOME_KV, fin_kv.at[others])
 
     merge = one_hot(row == jnp.where(col < HALF, 2 * col, 2 * col - (ROWS - 1)))
     quarter_low = iota((QUARTER, PAIR), 1) < HEAD_DIM
@@ -537,6 +527,8 @@
             parts.append(jnp.where(quarter_low, pltpu.roll(a, HEAD_DIM, 1), b))
         dq = jnp.concatenate(parts, axis=0).astype(BF16)
         out_ref[0, :, lanes] = dot(merge, dq).astype(BF16)
+    stores = [pltpu.make_async_copy(out_ref.at[0], out_hbm.at[0], load_sem.at[2])]
+    stores[0].start()
     tile_low = iota((TILE, PAIR), 1) < HEAD_DIM
     hits = []
     for h in range(HEADS):
@@ -545,8 +537,8 @@
         hits.append(((tile_row == off_ref[2, h] + tile_col * FEW) & (tile_col < 4)).astype(F32))
     hits = [jnp.concatenate(hits[i : i + 2], axis=1).astype(BF16) for i in range(0, HEADS, 2)]
 
-    for copy in few_copies:
-        copy.wait()
+    received(HOME2, fin_few.at[others])
+    sent(HOME2, fin_few.at[others])
     for t in range(HEADS // 2):
         lanes = slice(t * PAIR, (t + 1) * PAIR)
         a = fin_few[2 * t].astype(F32)
@@ -556,6 +548,12 @@
         for i, x in enumerate((dk, dv)):
             added = dot(hits[t], jnp.concatenate(x, axis=0).astype(BF16))
             out_ref[i + 1, :, lanes] = (base_kv[i, :, lanes] + added).astype(BF16)
+    stores.append(
+        pltpu.make_async_copy(out_ref.at[pl.ds(1, 2)], out_hbm.at[pl.ds(1, 2)], load_sem.at[3])
+    )
+    stores[1].start()
+    for store in stores:
+        store.wait()
 
 
 def local(queries, keys, values, grad_out, offsets):
@@ -569,13 +567,10 @@
         kernel,
         out_shape=jax.ShapeDtypeStruct((3, ROWS, width), BF16),
         in_specs=[pl.BlockSpec(memory_space=pltpu.HBM)] * 5,
-        out_specs=pl.BlockSpec(memory_space=pltpu.VMEM),
+        out_specs=pl.BlockSpec(memory_space=pltpu.HBM),
         scratch_shapes=[
             pltpu.SMEM((LEVELS, HEADS), jnp.int32),
-            low_buffer(ROWS, width),
-            low_buffer(ROWS, width),
-            low_buffer(ROWS, width),
-            low_buffer(ROWS, width),
+            low_buffer(4, ROWS, width),
             low_buffer(HEADS, TILE, PAIR),
             low_buffer(HEADS, 2, HALF, PAIR),
             low_buffer(HEADS, 2, HALF, PAIR),
@@ -603,17 +598,11 @@
             low_buffer(KEYS + WIDE, COLS),
             pltpu.VMEM((KEYS + WIDE, PAIR), F32),
             pltpu.VMEM((2, ROWS, width), F32),
-            dma((2, 2, GROUP)),
-            dma((2, GROUP)),
-            dma((2, 2, GROUP)),
-            dma((2, GROUP)),
-            dma((2, 3, MATES)),
-            dma((2, 3)),
-            dma((2, 2, GROUP)),
-            dma((2, GROUP)),
-            dma((2, GROUP)),
-            dma((2, GROUP)),
-            dma((5,)),
+            low_buffer(3, ROWS, width),
+            dma((KINDS,)),
+            dma((KINDS,)),
+            dma((4,)),
+            pltpu.SemaphoreType.REGULAR,
         ],
         compiler_params=pltpu.CompilerParams(
             collective_id=0, has_side_effects=True, vmem_limit_bytes=63 * 1024 * 1024

time: 41.2 us -> 38.6 us (0.937)
  Pallas kernels: 38.7 us -> 36 us
    pallas_call x1, Pallas kernels: 38.7 us -> 36 us  [local(): pl.pallas_call(kernel, out_shape=jax.ShapeDtypeStruct((3, ROWS, width), B...]
where the time goes in v2:
time: 38.6 us; the launch traced here: 38.4 us
  Pallas kernels  36 us (93%)
  local copies, waits for them, and re-layouts  1.78 us (5%)
  between operations  0.64 us (2%)
    pallas_call x1, Pallas kernels, local(): pl.pallas_call(kernel, out_shape=jax.ShapeDtypeStruct((3, ROWS, width), B...  36 us
    squeeze x1, local copies, waits for them, and re-layouts, local(): return (result[0], result[1], result[2])  1.78 us

profile of v2, /device:TPU:1, one launch (start us, length us, event | category | flops | bytes accessed | tf_op | source)
XLA Modules:
  0.0 38.4 jit_solution(16753960966056397254)
XLA Ops:
  0.6 36.0 %shard_map.76 = bf16[3,128,512]{2,1,0:T(8,128)(2,1)} custom-call(s32[3,8]{1,0:T(4,128)} %off_hbm.1, bf16[128,512]{1,0:T(8,128)(2,1)} %q_hbm.1, bf16[128,512]{1,0:T(8,128)(2,1)} %k_hbm.1, bf16[128,512]{1,0:T(8,128)(2,1)} %v_hbm.1, bf16[128,512]{1,0:T(8,128)(2,1)} %g_hbm.1), custom_call_target="tpu_custom_call" | custom-call | tf_op jit(solution)/shard_map/pallas_call | solution.py:566
  36.7 1.8 %slice_bitcast_fusion = (bf16[128,512]{1,0:T(8,128)(2,1)}, bf16[128,512]{1,0:T(8,128)(2,1)}, bf16[128,512]{1,0:T(8,128)(2,1)}) fusion(bf16[3,128,512]{2,1,0:T(8,128)(2,1)} %shard_map.76), kind=kLoop, calls=%fused_computation | loop fusion | bytes 786432 | tf_op jit(solution)/shard_map/squeeze | solution.py:611

commit v3 on v2

v3 whole, which is shorter than its diff:
```python
import math

import jax
import jax.numpy as jnp
from jax import lax
from jax.experimental import pallas as pl
from jax.experimental.pallas import tpu as pltpu
from jax.sharding import PartitionSpec as P

HEADS = 8
HEAD_DIM = 64
KEYS = 1024
LEVELS = 3
ROWS = 128
HALF = ROWS // 2
GROUP = 8
MATES = 16
WIDE = 512
FEW = 32
TILE = 16
PAIR = 2 * HEAD_DIM
SCALE = HEAD_DIM ** (-0.5)
TO_EXP2 = SCALE * math.log2(math.e)
LOWEST = -1e30
MESH = pl.DeviceIdType.MESH
F32 = jnp.float32
BF16 = jnp.bfloat16
COLS = 256
SLOTS = COLS // HALF
DEEP = 128
HOME_ROWS = ROWS + HALF + HALF + TILE
KINDS = 18
(
    FEW_OWN,
    FEW_PAIRED,
    KV,
    LEVEL1,
    QG,
    GATHER,
    PASS,
    STAT,
    HOME_DQ,
    HOME_KV,
    HOME1,
    HOME2,
) = (0, 1, 2, 3, 4, 8, 10, 12, 13, 15, 16, 17)
FAR_FIRST = (6, 2, 5, 7, 4, 1, 3)
LAYERS = 8
NEAR_LAYERS = (2, 6, 1, 7)
LAYERS_FAR_FIRST = (4, 3, 5, 2, 6, 1, 7)
MATES_FAR_FIRST = (9, 8, 7, 10, 6, 11, 5, 12, 4, 13, 3, 14, 2, 15, 1)


def dot(x, y):
    return jnp.dot(x, y, preferred_element_type=F32)


def dot_nt(x, y):
    return lax.dot_general(x, y, (((1,), (1,)), ((), ())), preferred_element_type=F32)


def iota(shape, dim):
    return lax.broadcasted_iota(jnp.int32, shape, dim)


def one_hot(hit):
    return hit.astype(F32).astype(BF16)


def two_parts(x):
    high = x.astype(BF16)
    return high, (x - high.astype(F32)).astype(BF16)


def fold8(x, op):
    parts = [x[8 * i : 8 * i + 8] for i in range(x.shape[0] // 8)]
    while len(parts) > 1:
        parts = [op(parts[i], parts[i + 1]) for i in range(0, len(parts), 2)]
    return parts[0]


def kernel(
    off_hbm,
    q_hbm,
    k_hbm,
    v_hbm,
    g_hbm,
    fin,
    off_ref,
    in_ref,
    send_few,
    send_kv,
    send_qg,
    few,
    few1,
    kv,
    qg,
    peer,
    keys2,
    rows2,
    stats2,
    k_t,
    out_kv,
    out_q,
    out_l1,
    out_few,
    score,
    dprob,
    dsc,
    dq_t,
    acc,
    send_sem,
    recv_sem,
    load_sem,
    own_sem,
    hop_sem,
):
    loads = [
        pltpu.make_async_copy(src, in_ref.at[i], load_sem.at[0])
        for i, src in enumerate((k_hbm, v_hbm, q_hbm, g_hbm))
    ]
    loads.append(pltpu.make_async_copy(off_hbm, off_ref, load_sem.at[1]))
    for load in loads:
        load.start()

    major = lax.axis_index("ctxa")
    minor = lax.axis_index("ctxb")
    head = minor % GROUP
    mate = (major // 2) * 4 + minor // GROUP

    def member(dx, dy):
        x = (head % 4 + dx) % 4
        y = (head // 4 + dy) % 2
        return y * 4 + x

    def at_head(other):
        return (major, (minor // GROUP) * GROUP + other)

    def at_mate(other, flip=0):
        return ((other // 4) * 2 + (major + flip) % 2, (other % 4) * GROUP + head)

    layer = mate // 2

    def at_layer(other):
        return ((other // 2) * 2 + major % 2, (other % 2) * (2 * GROUP) + minor % (2 * GROUP))

    ahead = [member(r % 4, r // 4) for r in range(GROUP)]
    behind = [member(4 - r % 4, r // 4) for r in range(GROUP)]
    sibling = (major + 1 - 2 * (major % 2), minor)
    paired = minor // GROUP + 1 - 2 * ((minor // GROUP) % 2)

    def at_paired(other):
        return (major, paired * GROUP + other)

    def send(src, dst, kind, device):
        pltpu.make_async_remote_copy(
            src_ref=src,
            dst_ref=dst,
            send_sem=send_sem.at[kind],
            recv_sem=recv_sem.at[kind],
            device_id=device,
            device_id_type=MESH,
        ).start()

    def received(kind, amount):
        pltpu.make_async_copy(amount, amount, recv_sem.at[kind]).wait()

    def sent(kind, amount):
        pltpu.make_async_copy(amount, amount, send_sem.at[kind]).wait()

    barrier = pltpu.get_barrier_semaphore()

    def greet(device):
        pl.semaphore_signal(barrier, inc=1, device_id=device, device_id_type=MESH)

    for r in FAR_FIRST:
        greet(at_head(ahead[r]))
    for r in (*FAR_FIRST, 0):
        greet(at_paired(behind[r]))
    for r in NEAR_LAYERS:
        greet(at_layer((layer + r) % LAYERS))
    greet(sibling)
    row = iota((ROWS, ROWS), 0)
    col = iota((ROWS, ROWS), 1)
    split = one_hot(col == jnp.where(row < HALF, 2 * row, 2 * row - (ROWS - 1)))
    low = iota((ROWS, PAIR), 1) < HEAD_DIM

    pltpu.make_async_copy(in_ref, in_ref, load_sem.at[0]).wait()
    loads[4].wait()
    order = [[None, None] for _ in range(HEADS)]
    for which, packed in enumerate((send_kv, send_qg)):
        x_all = dot(split, in_ref[2 * which])
        y_all = dot(split, in_ref[2 * which + 1])
        for t in range(HEADS // 2):
            x = x_all[:, t * PAIR : (t + 1) * PAIR]
            y = y_all[:, t * PAIR : (t + 1) * PAIR]
            for h, both in (
                (2 * t, jnp.where(low, x, pltpu.roll(y, HEAD_DIM, 1))),
                (2 * t + 1, jnp.where(low, pltpu.roll(x, HEAD_DIM, 1), y)),
            ):
                even = off_ref[1, h] == 0
                first = jnp.where(even, both[:HALF], both[HALF:]).astype(BF16)
                second = jnp.where(even, both[HALF:], both[:HALF]).astype(BF16)
                packed[h, 0] = first
                packed[h, 1] = second
                order[h][which] = [first, second]
    tile_row = iota((TILE, 2 * ROWS), 0)
    tile_col = iota((TILE, 2 * ROWS), 1)
    wanted = (tile_row >> 2) * ROWS + (tile_row & 3) * 16
    for h in range(HEADS):
        place = ((off_ref[1, h] + off_ref[2, h]) % 2) * HALF + (off_ref[2, h] >> 1)
        hit = one_hot((tile_col == wanted + place) & (tile_row < 8))
        send_few[h] = dot(hit, jnp.concatenate(order[h][0] + order[h][1], axis=0)).astype(BF16)

    pl.semaphore_wait(barrier, GROUP - 1 + GROUP + len(NEAR_LAYERS) + 1)

    for r in FAR_FIRST:
        tile = few.at[pl.ds(r * TILE, TILE), :]
        send(send_few.at[ahead[r]], tile, FEW_OWN, at_head(ahead[r]))
    for r in (*FAR_FIRST, 0):
        tile = few1.at[pl.ds(r * TILE, TILE), :]
        send(send_few.at[ahead[r]], tile, FEW_PAIRED, at_paired(ahead[r]))
    for r in NEAR_LAYERS[:2]:
        pl.semaphore_signal(
            hop_sem,
            inc=1,
            device_id=at_layer((layer + r) % LAYERS),
            device_id_type=MESH,
        )
    for r in FAR_FIRST:
        slot = kv.at[:, pl.ds(r * HALF, HALF), :]
        send(send_kv.at[ahead[r]], slot, KV, at_head(ahead[r]))
    for r in (*FAR_FIRST, 0):
        slot = peer.at[pl.ds(r * HALF, HALF), :]
        send(send_kv.at[ahead[r], 0], slot, LEVEL1, at_paired(ahead[r]))

    def block_kind(c):
        return QG + c

    for half in (0, 1):
        for r in FAR_FIRST:
            slot = qg.at[half, pl.ds(r * HALF, HALF), :]
            kind = block_kind(2 * half + r // SLOTS)
            send(send_qg.at[ahead[r], half], slot, kind, at_head(ahead[r]))
    few[:TILE] = send_few[head]
    kv[:, :HALF] = send_kv[head]
    qg[:, :HALF] = send_qg[head]

    off1 = off_ref[1, head]
    off2 = off_ref[2, head]
    inside = (off1 + off2) % 2 == 0
    base = jnp.where(inside, 0, WIDE) + (off2 >> 1)
    at = iota((FEW, KEYS), 0)
    pick = iota((FEW, KEYS), 1) == base + (at >> 2) * HALF + (at & 3) * 16
    at = iota((KEYS, FEW), 1)
    pick_t = one_hot(iota((KEYS, FEW), 0) == base + (at >> 2) * HALF + (at & 3) * 16)
    pick_low = one_hot(pick)
    at = iota((2 * FEW, GROUP * TILE), 0)
    gather = one_hot(
        iota((2 * FEW, GROUP * TILE), 1)
        == ((at % FEW) >> 2) * TILE + (at & 3) + jnp.where(at < FEW, 0, 4)
    )
    pl.semaphore_wait(hop_sem, 2)
    received(FEW_OWN, few.at[pl.ds(TILE, (GROUP - 1) * TILE)])
    received(FEW_PAIRED, few1)
    picked = dot(gather, few[...])
    picked1 = dot(gather, few1[...])
    own_kv2 = picked[:FEW]
    own_qg2 = picked[FEW:]
    mate1 = mate + 1 - 2 * (mate % 2)
    keys2[mate] = own_kv2.astype(BF16)
    rows2[mate] = own_qg2.astype(BF16)
    keys2[mate1] = picked1[:FEW].astype(BF16)
    rows2[mate1] = picked1[FEW:].astype(BF16)
    block = keys2.at[pl.ds(layer * 2, 2)]
    for r in LAYERS_FAR_FIRST:
        send(block, block, GATHER, at_layer((layer + r) % LAYERS))
    other_layers = keys2.at[pl.ds(0, MATES - 2)]
    this_core = pl.ds(0, MATES)
    that_core = pl.ds(MATES, MATES)

    received(KV, kv.at[:, pl.ds(HALF, WIDE - HALF), :])
    lane_low = iota((1, PAIR), 1) < HEAD_DIM
    zero = jnp.zeros((), BF16)
    kv_all = kv[...].reshape(KEYS, PAIR)

    def block_slots(c):
        slots = SLOTS if c % 2 else SLOTS - 1
        return qg.at[c // 2, pl.ds(WIDE - COLS, slots * HALF), :]

    def key_rows(j):
        if j < KEYS:
            return kv[j // WIDE, j % WIDE : j % WIDE + DEEP]
        return peer[j - KEYS : j - KEYS + DEEP]

    def stats(c):
        half = c // 2
        first = (c % 2) * COLS
        across = qg[half, first : first + COLS, :].T
        across_low = iota((PAIR, COLS), 0) < HEAD_DIM
        across_q = jnp.where(across_low, across, zero)
        across_g = jnp.where(across_low, zero, across)
        steps = range(0, depth_of(c), DEEP)
        high8 = jnp.full((8, COLS), LOWEST, F32)
        for j in steps:
            s = dot(key_rows(j), across_q) * TO_EXP2
            score[c, j : j + DEEP] = s
            high8 = jnp.maximum(high8, fold8(s, jnp.maximum))
        high = jnp.max(high8, axis=0, keepdims=True)
        sum8 = jnp.zeros((8, COLS), F32)
        dot8 = jnp.zeros((8, COLS), F32)
        for j in steps:
            e = jnp.exp2(score[c, j : j + DEEP] - high)
            score[c, j : j + DEEP] = e
            d = dot(key_rows(j), across_g)
            dprob[c, j : j + DEEP] = d
            sum8 = sum8 + weight(c, j) * fold8(e, jnp.add)
            dot8 = dot8 + weight(c, j) * fold8(e * d, jnp.add)
        return (
            high,
            jnp.sum(sum8, axis=0, keepdims=True),
            jnp.sum(dot8, axis=0, keepdims=True),
        )

    def depth_of(c):
        return KEYS + WIDE if c < 2 else KEYS

    def weight(c, j):
        return 2.0 if c < 2 and j < WIDE else 1.0

    received(LEVEL1, peer)
    peer_all = peer[...]
    received(GATHER, other_layers)
    send(keys2.at[this_core], keys2.at[that_core], PASS, sibling)
    few_low = iota((FEW, PAIR), 1) < HEAD_DIM
    both2 = jnp.concatenate(
        [jnp.where(few_low, own_qg2, 0.0), jnp.where(few_low, 0.0, own_qg2)], axis=0
    ).astype(BF16)
    here = dot_nt(both2, kv_all)
    near = dot_nt(both2, peer_all)
    s_here = here[:FEW] * TO_EXP2
    s_near = jnp.where(inside, near[:FEW] * TO_EXP2, LOWEST)
    twice = jnp.where((iota((FEW, KEYS), 1) < WIDE) & inside, 2.0, 1.0)
    high_own = jnp.maximum(
        jnp.max(s_here, axis=1, keepdims=True), jnp.max(s_near, axis=1, keepdims=True)
    )
    e_here = jnp.exp2(s_here - high_own) * twice
    e_near = jnp.exp2(s_near - high_own)
    sum_own = jnp.sum(e_here, axis=1, keepdims=True) + jnp.sum(e_near, axis=1, keepdims=True)
    dot_own = jnp.sum(e_here * here[FEW:], axis=1, keepdims=True) + jnp.sum(
        e_near * near[FEW:], axis=1, keepdims=True
    )
    block = rows2.at[pl.ds(layer * 2, 2)]
    for r in LAYERS_FAR_FIRST:
        send(block, block, GATHER + 1, at_layer((layer + r) % LAYERS))
    for c in (0, 1):
        received(block_kind(c), block_slots(c))
    found = [stats(0), stats(1)]
    received(PASS, keys2.at[this_core])

    kv2 = keys2[...].reshape(KEYS, PAIR)
    far = dot_nt(both2, kv2)
    s2 = far[:FEW] * TO_EXP2
    d2 = far[FEW:]
    high2 = jnp.maximum(high_own, jnp.max(s2, axis=1, keepdims=True))
    e2 = jnp.exp2(s2 - high2)
    sum2 = jnp.sum(e2, axis=1, keepdims=True)
    dot2 = jnp.sum(e2 * d2, axis=1, keepdims=True)
    shift = jnp.exp2(high_own - high2)
    total2 = sum2 + shift * sum_own
    product2 = dot2 + shift * dot_own
    lse2 = high2 + jnp.log(total2) * math.log2(math.e)
    delta2 = product2 / total2
    lanes = iota((FEW, PAIR), 1) == (mate % 4) * FEW + iota((FEW, PAIR), 0)
    stats2[mate] = jnp.concatenate(
        [
            jnp.sum(jnp.where(lanes, lse2, 0.0), axis=0, keepdims=True),
            jnp.sum(jnp.where(lanes, delta2, 0.0), axis=0, keepdims=True),
        ],
        axis=0,
    )
    stat_block = stats2.at[mate]
    stat_block1 = stats2.at[MATES + mate]
    for r in MATES_FAR_FIRST:
        send(stat_block, stat_block, STAT, at_mate((mate + r) % MATES))
        send(stat_block, stat_block1, STAT, at_mate((mate + r) % MATES, 1))
    send(stat_block, stat_block1, STAT, sibling)
    other_stats = stats2.at[pl.ds(0, 2 * MATES - 1)]
    ds2 = jnp.exp2(s2 - lse2) * (d2 - delta2)
    dq2_parts = two_parts(dot(ds2.astype(BF16), kv2).T[:HEAD_DIM])

    high2_row = jnp.max(jnp.where(pick, high2, LOWEST), axis=0, keepdims=True)
    sum2_row = jnp.sum(jnp.where(pick, sum2, 0.0), axis=0, keepdims=True)
    dot2_row = jnp.sum(jnp.where(pick, dot2, 0.0), axis=0, keepdims=True)

    def grads(c, own):
        columns = slice(c * COLS, (c + 1) * COLS)
        high, total, product = own
        top = jnp.maximum(high, high2_row[:, columns])
        factor = jnp.exp2(high - top)
        factor2 = jnp.exp2(high2_row[:, columns] - top)
        inverse = 1.0 / (factor * total + factor2 * sum2_row[:, columns])
        delta = (factor * product + factor2 * dot2_row[:, columns]) * inverse
        factor = factor * inverse
        mine = qg[c // 2, (c % 2) * COLS : (c % 2 + 1) * COLS, :]
        scaled_q = jnp.where(lane_low, mine * jnp.asarray(SCALE, BF16), zero)
        only_g = jnp.where(lane_low, zero, mine)
        depth = depth_of(c)
        for j in range(0, depth, DEEP):
            p = score[c, j : j + DEEP] * (weight(c, j) * factor)
            ds = (p * (dprob[c, j : j + DEEP] - delta)).astype(BF16)
            dsc[c, j : j + DEEP] = ds
            added = dot(ds, scaled_q) + dot(p.astype(BF16), only_g)
            acc[j : j + DEEP] = added if c == 0 else acc[j : j + DEEP] + added
        dq_t[c // 2, :, (c % 2) * COLS : (c % 2 + 1) * COLS] = dot(k_t[:, :depth], dsc[c, :depth])

    def dq_home(half):
        columns = slice(half * WIDE, (half + 1) * WIDE)
        dq = dq_t[half] + dot(dq2_parts[0], pick_low[:, columns])
        dq = (dq + dot(dq2_parts[1], pick_low[:, columns])) * SCALE
        for i in range(0, WIDE, PAIR):
            two = jnp.concatenate([dq[:, i : i + PAIR], dq[:, i : i + PAIR]], axis=0).T
            for b in range(2):
                rows = two[b * HALF : (b + 1) * HALF]
                lanes_low = iota((HALF // 2, PAIR), 1) < HEAD_DIM
                out_q[half, i // HALF + b] = jnp.where(
                    lanes_low, rows[: HALF // 2], rows[HALF // 2 :]
                ).astype(BF16)
        place = pl.ds(ROWS + HALF + half * (HALF // 2), HALF // 2)
        for r in FAR_FIRST:
            send(out_q.at[half, r], fin.at[head, place], HOME_DQ + half, at_head(behind[r]))
        own = pltpu.make_async_copy(out_q.at[half, 0], fin.at[head, place], own_sem.at[half])
        own.start()
        return own

    k_t[:, :KEYS] = kv_all.T[:HEAD_DIM]
    k_t[:, KEYS:] = peer_all.T[:HEAD_DIM]
    grads(0, found[0])
    grads(1, found[1])
    out_l1[...] = acc[KEYS:].astype(BF16)
    for r in (*FAR_FIRST, 0):
        slot = out_l1.at[pl.ds(r * HALF, HALF), :]
        send(slot, fin.at[head, pl.ds(ROWS, HALF)], HOME1, at_paired(behind[r]))
    own_copies = [dq_home(0)]
    for c in (2, 3):
        received(block_kind(c), block_slots(c))
    found = [stats(2), stats(3)]
    grads(2, found[0])
    grads(3, found[1])
    for r in range(GROUP):
        for half in range(2):
            rows = slice(half * WIDE + r * HALF, half * WIDE + (r + 1) * HALF)
            out_kv[r, half * HALF : (half + 1) * HALF] = acc[rows].astype(BF16)
    for r in FAR_FIRST:
        send(out_kv.at[r], fin.at[head, pl.ds(0, ROWS)], HOME_KV, at_head(behind[r]))
    own_copies.append(
        pltpu.make_async_copy(out_kv.at[0], fin.at[head, pl.ds(0, ROWS)], own_sem.at[2])
    )
    own_copies[-1].start()
    received(GATHER + 1, other_layers)
    send(rows2.at[this_core], rows2.at[that_core], PASS + 1, sibling)
    own_copies.append(dq_home(1))

    received(PASS + 1, rows2.at[this_core])
    qg2 = rows2[...].reshape(KEYS, PAIR)
    back = dot_nt(
        jnp.concatenate(
            [jnp.where(few_low, own_kv2, 0.0), jnp.where(few_low, 0.0, own_kv2)], axis=0
        ).astype(BF16),
        qg2,
    )
    scaled_q2 = jnp.where(lane_low, qg2 * jnp.asarray(SCALE, BF16), zero)
    only_g2 = jnp.where(lane_low, zero, qg2)
    at = iota((GROUP * TILE, FEW), 0)
    deal = one_hot(
        (iota((GROUP * TILE, FEW), 1) == (at >> 4) * 4 + (at & (TILE - 1)))
        & ((at & (TILE - 1)) < 4)
    )
    received(STAT, other_stats)
    tiles = []
    for m in range(0, 2 * MATES, 4):
        tiles.append((stats2[m] + stats2[m + 1]) + (stats2[m + 2] + stats2[m + 3]))
    tiles = jnp.concatenate(tiles, axis=1)
    p2 = jnp.exp2(back[:FEW] * TO_EXP2 - tiles[0:1])
    ds2 = p2 * (back[FEW:] - tiles[1:2])
    kv_grad2 = dot(ds2.astype(BF16), scaled_q2) + dot(p2.astype(BF16), only_g2)
    out_few[...] = dot(deal, kv_grad2.astype(BF16)).astype(BF16)
    place = pl.ds(HOME_ROWS - TILE, TILE)
    for r in FAR_FIRST:
        tile = out_few.at[pl.ds(r * TILE, TILE), :]
        send(tile, fin.at[head, place], HOME2, at_head(behind[r]))
    own_copies.append(
        pltpu.make_async_copy(out_few.at[pl.ds(0, TILE), :], fin.at[head, place], own_sem.at[3])
    )
    own_copies[-1].start()

    sent(FEW_OWN, few.at[pl.ds(TILE, (GROUP - 1) * TILE)])
    sent(FEW_PAIRED, few1)
    sent(KV, kv.at[:, pl.ds(HALF, WIDE - HALF), :])
    sent(LEVEL1, peer)
    for c in range(4):
        sent(block_kind(c), block_slots(c))
    sent(GATHER, other_layers)
    sent(GATHER + 1, other_layers)
    sent(PASS, keys2.at[this_core])
    sent(PASS + 1, rows2.at[this_core])
    sent(STAT, other_stats)

    for done in (received, sent):
        for half in range(2):
            done(HOME_DQ + half, out_q.at[half, pl.ds(1, GROUP - 1)])
        done(HOME1, out_l1)
        done(HOME_KV, out_kv.at[pl.ds(1, GROUP - 1)])
    for copy in own_copies:
        copy.wait()
    for done in (received, sent):
        done(HOME2, out_few.at[pl.ds(TILE, (GROUP - 1) * TILE), :])


def finish(off_hbm, fin_hbm, dq_hbm, dk_hbm, dv_hbm, off_ref, fin, held, load_sem, store_sem):
    loads = [
        pltpu.make_async_copy(fin_hbm.at[pl.ds(h, 2)], fin.at[pl.ds(h, 2)], load_sem.at[h // 2])
        for h in range(0, HEADS, 2)
    ]
    loads.append(pltpu.make_async_copy(off_hbm, off_ref, load_sem.at[HEADS // 2]))
    for load in loads:
        load.start()
    row = iota((ROWS, ROWS), 0)
    col = iota((ROWS, ROWS), 1)
    merge = one_hot(row == jnp.where(col < HALF, 2 * col, 2 * col - (ROWS - 1)))
    low = iota((ROWS, PAIR), 1) < HEAD_DIM
    half_low = iota((HALF, PAIR), 1) < HEAD_DIM
    tile_row = iota((ROWS, TILE), 0)
    tile_col = iota((ROWS, TILE), 1)
    loads[-1].wait()

    def ordered(h, first, second):
        even = off_ref[1, h] == 0
        return jnp.where(even, first, second), jnp.where(even, second, first)

    def ordered_kv(h):
        place = ((off_ref[1, h] + off_ref[2, h]) % 2) * HALF + (off_ref[2, h] >> 1)
        hit = one_hot((tile_row == place + tile_col * 16) & (tile_col < 4))
        level2 = dot(hit, fin[h, HOME_ROWS - TILE :])
        first = fin[h, :HALF].astype(F32) + fin[h, ROWS : ROWS + HALF].astype(F32) + level2[:HALF]
        second = fin[h, HALF:ROWS].astype(F32) + level2[HALF:]
        return jnp.concatenate(ordered(h, first, second), axis=0)

    def ordered_q(h, side):
        halves = []
        for half in range(2):
            start = ROWS + HALF + half * (HALF // 2)
            x = fin[h, start : start + HALF // 2].astype(F32)
            turned = pltpu.roll(x, HEAD_DIM, 1)
            halves.append(jnp.concatenate([turned, x] if side else [x, turned], axis=0))
        return ordered(h, *halves)

    for load in loads[:-1]:
        load.wait()
    stores = []

    def store(i, parts, result):
        for t, x in enumerate(parts):
            lanes = slice(t * PAIR, (t + 1) * PAIR)
            held[i, :, lanes] = dot(merge, x.astype(BF16)).astype(BF16)
        stores.append(pltpu.make_async_copy(held.at[i], result, store_sem.at[i]))
        stores[-1].start()

    parts = []
    for t in range(HEADS // 2):
        a = ordered_q(2 * t, 0)
        b = ordered_q(2 * t + 1, 1)
        both = [jnp.where(half_low, a[i], b[i]) for i in range(2)]
        parts.append(jnp.concatenate(both, axis=0))
    store(0, parts, dq_hbm)
    heads = [ordered_kv(h) for h in range(HEADS)]
    pairs = [(heads[h], heads[h + 1]) for h in range(0, HEADS, 2)]
    store(1, [jnp.where(low, a, pltpu.roll(b, HEAD_DIM, 1)) for a, b in pairs], dk_hbm)
    store(2, [jnp.where(low, pltpu.roll(a, HEAD_DIM, 1), b) for a, b in pairs], dv_hbm)
    for copy in stores:
        copy.wait()


def local(queries, keys, values, grad_out, offsets):
    width = HEADS * HEAD_DIM
    dma = pltpu.SemaphoreType.DMA

    def low_buffer(*shape):
        return pltpu.VMEM(shape, BF16)

    result = pl.pallas_call(
        kernel,
        out_shape=jax.ShapeDtypeStruct((HEADS, HOME_ROWS, PAIR), BF16),
        in_specs=[pl.BlockSpec(memory_space=pltpu.HBM)] * 5,
        out_specs=pl.BlockSpec(memory_space=pltpu.HBM),
        scratch_shapes=[
            pltpu.SMEM((LEVELS, HEADS), jnp.int32),
            low_buffer(4, ROWS, width),
            low_buffer(HEADS, TILE, PAIR),
            low_buffer(HEADS, 2, HALF, PAIR),
            low_buffer(HEADS, 2, HALF, PAIR),
            low_buffer(GROUP * TILE, PAIR),
            low_buffer(GROUP * TILE, PAIR),
            low_buffer(2, WIDE, PAIR),
            low_buffer(2, WIDE, PAIR),
            low_buffer(WIDE, PAIR),
            low_buffer(2 * MATES, FEW, PAIR),
            low_buffer(2 * MATES, FEW, PAIR),
            pltpu.VMEM((2 * MATES, 2, PAIR), F32),
            low_buffer(HEAD_DIM, KEYS + WIDE),
            low_buffer(GROUP, ROWS, PAIR),
            low_buffer(2, GROUP, HALF // 2, PAIR),
            low_buffer(WIDE, PAIR),
            low_buffer(GROUP * TILE, PAIR),
            pltpu.VMEM((4, KEYS + WIDE, COLS), F32),
            pltpu.VMEM((4, KEYS + WIDE, COLS), F32),
            low_buffer(4, KEYS + WIDE, COLS),
            pltpu.VMEM((2, HEAD_DIM, WIDE), F32),
            pltpu.VMEM((KEYS + WIDE, PAIR), F32),
            dma((KINDS,)),
            dma((KINDS,)),
            dma((2,)),
            dma((4,)),
            pltpu.SemaphoreType.REGULAR,
        ],
        compiler_params=pltpu.CompilerParams(
            collective_id=0, has_side_effects=True, vmem_limit_bytes=63 * 1024 * 1024
        ),
    )(offsets, queries, keys, values, grad_out)
    one = jax.ShapeDtypeStruct((ROWS, width), BF16)
    hbm = pl.BlockSpec(memory_space=pltpu.HBM)
    return pl.pallas_call(
        finish,
        out_shape=(one, one, one),
        in_specs=[hbm, hbm],
        out_specs=(hbm, hbm, hbm),
        scratch_shapes=[
            pltpu.SMEM((LEVELS, HEADS), jnp.int32),
            low_buffer(HEADS, HOME_ROWS, PAIR),
            low_buffer(3, ROWS, width),
            dma((HEADS // 2 + 1,)),
            dma((3,)),
        ],
        compiler_params=pltpu.CompilerParams(vmem_limit_bytes=63 * 1024 * 1024),
    )(offsets, result)


def solution(mesh):
    rows = P(("ctxa", "ctxb"), None)
    return jax.shard_map(
        local,
        mesh=mesh,
        in_specs=(rows, rows, rows, rows, P()),
        out_specs=(rows, rows, rows),
        check_vma=False,
    )
```

time: 38.6 us -> 35.9 us (0.930)
  local copies, waits for them, and re-layouts: 1.78 us -> 0 us
  Pallas kernels: 36 us -> 35.2 us
    squeeze x1 -> x0, local copies, waits for them, and re-layouts: 1.78 us -> none  [local(): return (result[0], result[1], result[2])]
    pallas_call x1 -> x2, Pallas kernels: 36 us -> 35.2 us  [the longest x1 32.8 us: local(): pl.pallas_call(kernel, out_shape=jax.ShapeDtypeStruct((HEADS, HOME_ROWS,...]
where the time goes in v3:
time: 35.9 us; the launch traced here: 35.8 us
  Pallas kernels  35.2 us (98%)
  between operations  0.64 us (2%)
    pallas_call x1, Pallas kernels, local(): pl.pallas_call(kernel, out_shape=jax.ShapeDtypeStruct((HEADS, HOME_ROWS,...  32.8 us
    pallas_call x1, Pallas kernels, local(): pl.pallas_call(finish, out_shape=(one, one, one), in_specs=[hbm, hbm], ou...  2.42 us

profile of v3, /device:TPU:1, one launch (start us, length us, event | category | flops | bytes accessed | tf_op | source)
XLA Modules:
  0.0 35.8 jit_solution(6907166761270693885)
XLA Ops:
  0.6 32.8 %shard_map.76.fin_hbm = bf16[8,272,128]{2,1,0:T(8,128)(2,1)} custom-call(s32[3,8]{1,0:T(4,128)} %off_hbm.3, bf16[128,512]{1,0:T(8,128)(2,1)} %q_hbm.1, bf16[128,512]{1,0:T(8,128)(2,1)} %k_hbm.1, bf16[128,512]{1,0:T(8,128)(2,1)} %v_hbm.1, bf16[128,512]{1,0:T(8,128)(2,1)} %g_hbm.1), custom_call_target="tpu_custom_call" | custom-call | tf_op jit(solution)/shard_map/pallas_call | solution.py:591
  33.4 2.4 %shard_map.77 = (bf16[128,512]{1,0:T(8,128)(2,1)}, bf16[128,512]{1,0:T(8,128)(2,1)}, bf16[128,512]{1,0:T(8,128)(2,1)}) custom-call(s32[3,8]{1,0:T(4,128)} %off_hbm.3, bf16[8,272,128]{2,1,0:T(8,128)(2,1)} %shard_map.76.fin_hbm), custom_call_target="tpu_custom_call" | custom-call | tf_op jit(solution)/shard_map/pallas_call | solution.py:632

commit v4 on v3

--- a/solution.py
+++ b/solution.py
@@ -28,8 +28,12 @@
 COLS = 256
 SLOTS = COLS // HALF
 DEEP = 128
-HOME_ROWS = ROWS + HALF + HALF + TILE
-KINDS = 18
+QUARTER = HALF // 2
+HOME_L1_ROW = ROWS
+HOME_DQ_ROW = HOME_L1_ROW + HALF
+HOME_L2_ROW = HOME_DQ_ROW + HALF
+HOME_ROWS = HOME_L2_ROW + TILE
+KINDS = 24
 (
     FEW_OWN,
     FEW_PAIRED,
@@ -37,13 +41,14 @@
     LEVEL1,
     QG,
     GATHER,
+    ROWS2,
     PASS,
     STAT,
     HOME_DQ,
     HOME_KV,
     HOME1,
     HOME2,
-) = (0, 1, 2, 3, 4, 8, 10, 12, 13, 15, 16, 17)
+) = (0, 1, 2, 3, 4, 8, 16, 17, 19, 20, 21, 22, 23)
 FAR_FIRST = (6, 2, 5, 7, 4, 1, 3)
 LAYERS = 8
 NEAR_LAYERS = (2, 6, 1, 7)
@@ -274,7 +279,8 @@
     rows2[mate1] = picked1[FEW:].astype(BF16)
     block = keys2.at[pl.ds(layer * 2, 2)]
     for r in LAYERS_FAR_FIRST:
-        send(block, block, GATHER, at_layer((layer + r) % LAYERS))
+        send(block, block, GATHER + layer, at_layer((layer + r) % LAYERS))
+    send(block, keys2.at[pl.ds(MATES + layer * 2, 2)], PASS, sibling)
     other_layers = keys2.at[pl.ds(0, MATES - 2)]
     this_core = pl.ds(0, MATES)
     that_core = pl.ds(MATES, MATES)
@@ -330,8 +336,11 @@
 
     received(LEVEL1, peer)
     peer_all = peer[...]
-    received(GATHER, other_layers)
-    send(keys2.at[this_core], keys2.at[that_core], PASS, sibling)
+    for i in range(LAYERS - 1):
+        other = i + (i + LAYERS - layer) // LAYERS
+        block = keys2.at[pl.ds(other * 2, 2)]
+        received(GATHER + other, block)
+        send(block, keys2.at[pl.ds(MATES + other * 2, 2)], PASS, sibling)
     few_low = iota((FEW, PAIR), 1) < HEAD_DIM
     both2 = jnp.concatenate(
         [jnp.where(few_low, own_qg2, 0.0), jnp.where(few_low, 0.0, own_qg2)], axis=0
@@ -352,10 +361,12 @@
     )
     block = rows2.at[pl.ds(layer * 2, 2)]
     for r in LAYERS_FAR_FIRST:
-        send(block, block, GATHER + 1, at_layer((layer + r) % LAYERS))
+        send(block, block, ROWS2, at_layer((layer + r) % LAYERS))
     for c in (0, 1):
         received(block_kind(c), block_slots(c))
     found = [stats(0), stats(1)]
+    k_t[:, :KEYS] = kv_all.T[:HEAD_DIM]
+    k_t[:, KEYS:] = peer_all.T[:HEAD_DIM]
     received(PASS, keys2.at[this_core])
 
     kv2 = keys2[...].reshape(KEYS, PAIR)
@@ -386,9 +397,6 @@
         send(stat_block, stat_block1, STAT, at_mate((mate + r) % MATES, 1))
     send(stat_block, stat_block1, STAT, sibling)
     other_stats = stats2.at[pl.ds(0, 2 * MATES - 1)]
-    ds2 = jnp.exp2(s2 - lse2) * (d2 - delta2)
-    dq2_parts = two_parts(dot(ds2.astype(BF16), kv2).T[:HEAD_DIM])
-
     high2_row = jnp.max(jnp.where(pick, high2, LOWEST), axis=0, keepdims=True)
     sum2_row = jnp.sum(jnp.where(pick, sum2, 0.0), axis=0, keepdims=True)
     dot2_row = jnp.sum(jnp.where(pick, dot2, 0.0), axis=0, keepdims=True)
@@ -414,53 +422,51 @@
             acc[j : j + DEEP] = added if c == 0 else acc[j : j + DEEP] + added
         dq_t[c // 2, :, (c % 2) * COLS : (c % 2 + 1) * COLS] = dot(k_t[:, :depth], dsc[c, :depth])
 
-    def dq_home(half):
+    def dq_pack(half):
         columns = slice(half * WIDE, (half + 1) * WIDE)
         dq = dq_t[half] + dot(dq2_parts[0], pick_low[:, columns])
         dq = (dq + dot(dq2_parts[1], pick_low[:, columns])) * SCALE
+        lanes_low = iota((QUARTER, PAIR), 1) < HEAD_DIM
         for i in range(0, WIDE, PAIR):
             two = jnp.concatenate([dq[:, i : i + PAIR], dq[:, i : i + PAIR]], axis=0).T
             for b in range(2):
                 rows = two[b * HALF : (b + 1) * HALF]
-                lanes_low = iota((HALF // 2, PAIR), 1) < HEAD_DIM
-                out_q[half, i // HALF + b] = jnp.where(
-                    lanes_low, rows[: HALF // 2], rows[HALF // 2 :]
-                ).astype(BF16)
-        place = pl.ds(ROWS + HALF + half * (HALF // 2), HALF // 2)
-        for r in FAR_FIRST:
-            send(out_q.at[half, r], fin.at[head, place], HOME_DQ + half, at_head(behind[r]))
-        own = pltpu.make_async_copy(out_q.at[half, 0], fin.at[head, place], own_sem.at[half])
-        own.start()
-        return own
-
-    k_t[:, :KEYS] = kv_all.T[:HEAD_DIM]
-    k_t[:, KEYS:] = peer_all.T[:HEAD_DIM]
+                packed = jnp.where(lanes_low, rows[:QUARTER], rows[QUARTER:]).astype(BF16)
+                out_q[i // HALF + b, half * QUARTER : (half + 1) * QUARTER] = packed
+
     grads(0, found[0])
     grads(1, found[1])
     out_l1[...] = acc[KEYS:].astype(BF16)
     for r in (*FAR_FIRST, 0):
         slot = out_l1.at[pl.ds(r * HALF, HALF), :]
-        send(slot, fin.at[head, pl.ds(ROWS, HALF)], HOME1, at_paired(behind[r]))
-    own_copies = [dq_home(0)]
+        send(slot, fin.at[head, pl.ds(HOME_L1_ROW, HALF)], HOME1, at_paired(behind[r]))
+
+    def take_home(i, src, first, rows, kind):
+        place = fin.at[head, pl.ds(first, rows)]
+        for r in FAR_FIRST:
+            send(src.at[r], place, kind, at_head(behind[r]))
+        copy = pltpu.make_async_copy(src.at[0], place, own_sem.at[i])
+        copy.start()
+        return copy
+
+    received(ROWS2, other_layers)
+    send(rows2.at[this_core], rows2.at[that_core], PASS + 1, sibling)
     for c in (2, 3):
         received(block_kind(c), block_slots(c))
-    found = [stats(2), stats(3)]
-    grads(2, found[0])
-    grads(3, found[1])
+    found += [stats(2), stats(3)]
+    grads(2, found[2])
+    grads(3, found[3])
     for r in range(GROUP):
         for half in range(2):
             rows = slice(half * WIDE + r * HALF, half * WIDE + (r + 1) * HALF)
             out_kv[r, half * HALF : (half + 1) * HALF] = acc[rows].astype(BF16)
-    for r in FAR_FIRST:
-        send(out_kv.at[r], fin.at[head, pl.ds(0, ROWS)], HOME_KV, at_head(behind[r]))
-    own_copies.append(
-        pltpu.make_async_copy(out_kv.at[0], fin.at[head, pl.ds(0, ROWS)], own_sem.at[2])
-    )
-    own_copies[-1].start()
-    received(GATHER + 1, other_layers)
-    send(rows2.at[this_core], rows2.at[that_core], PASS + 1, sibling)
-    own_copies.append(dq_home(1))
-
+    own_copies = [take_home(0, out_kv, 0, ROWS, HOME_KV)]
+    ds2 = jnp.exp2(s2 - lse2) * (d2 - delta2)
+    dq2_parts = two_parts(dot(ds2.astype(BF16), kv2).T[:HEAD_DIM])
+
+    for half in range(2):
+        dq_pack(half)
+    own_copies.append(take_home(1, out_q, HOME_DQ_ROW, HALF, HOME_DQ))
     received(PASS + 1, rows2.at[this_core])
     qg2 = rows2[...].reshape(KEYS, PAIR)
     back = dot_nt(
@@ -484,15 +490,10 @@
     p2 = jnp.exp2(back[:FEW] * TO_EXP2 - tiles[0:1])
     ds2 = p2 * (back[FEW:] - tiles[1:2])
     kv_grad2 = dot(ds2.astype(BF16), scaled_q2) + dot(p2.astype(BF16), only_g2)
-    out_few[...] = dot(deal, kv_grad2.astype(BF16)).astype(BF16)
-    place = pl.ds(HOME_ROWS - TILE, TILE)
-    for r in FAR_FIRST:
-        tile = out_few.at[pl.ds(r * TILE, TILE), :]
-        send(tile, fin.at[head, place], HOME2, at_head(behind[r]))
-    own_copies.append(
-        pltpu.make_async_copy(out_few.at[pl.ds(0, TILE), :], fin.at[head, place], own_sem.at[3])
-    )
-    own_copies[-1].start()
+    dealt = dot(deal, kv_grad2.astype(BF16)).astype(BF16)
+    for r in range(GROUP):
+        out_few[r] = dealt[r * TILE : (r + 1) * TILE]
+    own_copies.append(take_home(2, out_few, HOME_L2_ROW, TILE, HOME2))
 
     sent(FEW_OWN, few.at[pl.ds(TILE, (GROUP - 1) * TILE)])
     sent(FEW_PAIRED, few1)
@@ -500,29 +501,33 @@
     sent(LEVEL1, peer)
     for c in range(4):
         sent(block_kind(c), block_slots(c))
-    sent(GATHER, other_layers)
-    sent(GATHER + 1, other_layers)
+    sent(GATHER + layer, other_layers)
+    sent(ROWS2, other_layers)
     sent(PASS, keys2.at[this_core])
     sent(PASS + 1, rows2.at[this_core])
     sent(STAT, other_stats)
 
     for done in (received, sent):
-        for half in range(2):
-            done(HOME_DQ + half, out_q.at[half, pl.ds(1, GROUP - 1)])
+        done(HOME_DQ, out_q.at[pl.ds(1, GROUP - 1)])
         done(HOME1, out_l1)
         done(HOME_KV, out_kv.at[pl.ds(1, GROUP - 1)])
     for copy in own_copies:
         copy.wait()
     for done in (received, sent):
-        done(HOME2, out_few.at[pl.ds(TILE, (GROUP - 1) * TILE), :])
+        done(HOME2, out_few.at[pl.ds(1, GROUP - 1)])
 
 
 def finish(off_hbm, fin_hbm, dq_hbm, dk_hbm, dv_hbm, off_ref, fin, held, load_sem, store_sem):
-    loads = [
-        pltpu.make_async_copy(fin_hbm.at[pl.ds(h, 2)], fin.at[pl.ds(h, 2)], load_sem.at[h // 2])
-        for h in range(0, HEADS, 2)
-    ]
-    loads.append(pltpu.make_async_copy(off_hbm, off_ref, load_sem.at[HEADS // 2]))
+    parts = (
+        (HOME_DQ_ROW, HALF),
+        (HOME_L2_ROW, TILE),
+        (HOME_L1_ROW, HALF),
+        (0, ROWS),
+    )
+    loads = [pltpu.make_async_copy(off_hbm, off_ref, load_sem.at[len(parts)])]
+    for i, (first, rows) in enumerate(parts):
+        block = (slice(None), pl.ds(first, rows))
+        loads.append(pltpu.make_async_copy(fin_hbm.at[block], fin.at[block], load_sem.at[i]))
     for load in loads:
         load.start()
     row = iota((ROWS, ROWS), 0)
@@ -532,7 +537,7 @@
     half_low = iota((HALF, PAIR), 1) < HEAD_DIM
     tile_row = iota((ROWS, TILE), 0)
     tile_col = iota((ROWS, TILE), 1)
-    loads[-1].wait()
+    loads[0].wait()
 
     def ordered(h, first, second):
         even = off_ref[1, h] == 0
@@ -541,22 +546,20 @@
     def ordered_kv(h):
         place = ((off_ref[1, h] + off_ref[2, h]) % 2) * HALF + (off_ref[2, h] >> 1)
         hit = one_hot((tile_row == place + tile_col * 16) & (tile_col < 4))
-        level2 = dot(hit, fin[h, HOME_ROWS - TILE :])
-        first = fin[h, :HALF].astype(F32) + fin[h, ROWS : ROWS + HALF].astype(F32) + level2[:HALF]
+        level2 = dot(hit, fin[h, HOME_L2_ROW:])
+        first = fin[h, :HALF].astype(F32) + fin[h, HOME_L1_ROW : HOME_L1_ROW + HALF].astype(F32) + level2[:HALF]
         second = fin[h, HALF:ROWS].astype(F32) + level2[HALF:]
         return jnp.concatenate(ordered(h, first, second), axis=0)
 
     def ordered_q(h, side):
         halves = []
-        for half in range(2):
-            start = ROWS + HALF + half * (HALF // 2)
-            x = fin[h, start : start + HALF // 2].astype(F32)
+        for start in (HOME_DQ_ROW, HOME_DQ_ROW + QUARTER):
+            x = fin[h, start : start + QUARTER].astype(F32)
             turned = pltpu.roll(x, HEAD_DIM, 1)
             halves.append(jnp.concatenate([turned, x] if side else [x, turned], axis=0))
         return ordered(h, *halves)
 
-    for load in loads[:-1]:
-        load.wait()
+    loads[1].wait()
     stores = []
 
     def store(i, parts, result):
@@ -573,6 +576,8 @@
         both = [jnp.where(half_low, a[i], b[i]) for i in range(2)]
         parts.append(jnp.concatenate(both, axis=0))
     store(0, parts, dq_hbm)
+    for load in loads[2:]:
+        load.wait()
     heads = [ordered_kv(h) for h in range(HEADS)]
     pairs = [(heads[h], heads[h + 1]) for h in range(0, HEADS, 2)]
     store(1, [jnp.where(low, a, pltpu.roll(b, HEAD_DIM, 1)) for a, b in pairs], dk_hbm)
@@ -609,9 +614,9 @@
             pltpu.VMEM((2 * MATES, 2, PAIR), F32),
             low_buffer(HEAD_DIM, KEYS + WIDE),
             low_buffer(GROUP, ROWS, PAIR),
-            low_buffer(2, GROUP, HALF // 2, PAIR),
+            low_buffer(GROUP, HALF, PAIR),
             low_buffer(WIDE, PAIR),
-            low_buffer(GROUP * TILE, PAIR),
+            low_buffer(GROUP, TILE, PAIR),
             pltpu.VMEM((4, KEYS + WIDE, COLS), F32),
             pltpu.VMEM((4, KEYS + WIDE, COLS), F32),
             low_buffer(4, KEYS + WIDE, COLS),
@@ -620,7 +625,7 @@
             dma((KINDS,)),
             dma((KINDS,)),
             dma((2,)),
-            dma((4,)),
+            dma((3,)),
             pltpu.SemaphoreType.REGULAR,
         ],
         compiler_params=pltpu.CompilerParams(
@@ -638,7 +643,7 @@
             pltpu.SMEM((LEVELS, HEADS), jnp.int32),
             low_buffer(HEADS, HOME_ROWS, PAIR),
             low_buffer(3, ROWS, width),
-            dma((HEADS // 2 + 1,)),
+            dma((5,)),
             dma((3,)),
         ],
         compiler_params=pltpu.CompilerParams(vmem_limit_bytes=63 * 1024 * 1024),

time: 35.9 us -> 35.9 us (level)
  no operation moved by 1% of the time
where the time goes in v4:
time: 35.9 us; the launch traced here: 35.7 us
  Pallas kernels  35 us (97%)
  between operations  0.64 us (2%)
    pallas_call x1, Pallas kernels, local(): pl.pallas_call(kernel, out_shape=jax.ShapeDtypeStruct((HEADS, HOME_ROWS,...  32.6 us
    pallas_call x1, Pallas kernels, local(): pl.pallas_call(finish, out_shape=(one, one, one), in_specs=[hbm, hbm], ou...  2.4 us

profile of v4, /device:TPU:1, one launch (start us, length us, event | category | flops | bytes accessed | tf_op | source)
XLA Modules:
  0.0 35.7 jit_solution(18043288345072962525)
XLA Ops:
  0.6 32.6 %shard_map.76.fin_hbm = bf16[8,272,128]{2,1,0:T(8,128)(2,1)} custom-call(s32[3,8]{1,0:T(4,128)} %off_hbm.3, bf16[128,512]{1,0:T(8,128)(2,1)} %q_hbm.1, bf16[128,512]{1,0:T(8,128)(2,1)} %k_hbm.1, bf16[128,512]{1,0:T(8,128)(2,1)} %v_hbm.1, bf16[128,512]{1,0:T(8,128)(2,1)} %g_hbm.1), custom_call_target="tpu_custom_call" | custom-call | tf_op jit(solution)/shard_map/pallas_call | solution.py:596
  33.3 2.4 %shard_map.77 = (bf16[128,512]{1,0:T(8,128)(2,1)}, bf16[128,512]{1,0:T(8,128)(2,1)}, bf16[128,512]{1,0:T(8,128)(2,1)}) custom-call(s32[3,8]{1,0:T(4,128)} %off_hbm.3, bf16[8,272,128]{2,1,0:T(8,128)(2,1)} %shard_map.76.fin_hbm), custom_call_target="tpu_custom_call" | custom-call | tf_op jit(solution)/shard_map/pallas_call | solution.py:637

commit v5 on v4

--- a/solution.py
+++ b/solution.py
@@ -535,21 +535,42 @@
     merge = one_hot(row == jnp.where(col < HALF, 2 * col, 2 * col - (ROWS - 1)))
     low = iota((ROWS, PAIR), 1) < HEAD_DIM
     half_low = iota((HALF, PAIR), 1) < HEAD_DIM
-    tile_row = iota((ROWS, TILE), 0)
-    tile_col = iota((ROWS, TILE), 1)
+    tile_low = iota((TILE, PAIR), 1) < HEAD_DIM
     loads[0].wait()
 
     def ordered(h, first, second):
         even = off_ref[1, h] == 0
         return jnp.where(even, first, second), jnp.where(even, second, first)
 
+    def merge_with_level2(t):
+        to = iota((ROWS, ROWS + 2 * TILE), 0)
+        at = iota((ROWS, ROWS + 2 * TILE), 1)
+        hit = to == jnp.where(at < HALF, 2 * at, 2 * at - (ROWS - 1))
+        hit = hit & (at < ROWS)
+        for i in range(2):
+            tile = at - (ROWS + i * TILE)
+            row = off_ref[2, 2 * t + i] + tile * FEW
+            hit = hit | ((to == row) & (tile >= 0) & (tile < 4))
+        return one_hot(hit)
+
     def ordered_kv(h):
-        place = ((off_ref[1, h] + off_ref[2, h]) % 2) * HALF + (off_ref[2, h] >> 1)
-        hit = one_hot((tile_row == place + tile_col * 16) & (tile_col < 4))
-        level2 = dot(hit, fin[h, HOME_L2_ROW:])
-        first = fin[h, :HALF].astype(F32) + fin[h, HOME_L1_ROW : HOME_L1_ROW + HALF].astype(F32) + level2[:HALF]
-        second = fin[h, HALF:ROWS].astype(F32) + level2[HALF:]
-        return jnp.concatenate(ordered(h, first, second), axis=0)
+        first = fin[h, :HALF].astype(F32) + fin[h, HOME_L1_ROW : HOME_L1_ROW + HALF].astype(F32)
+        return jnp.concatenate(ordered(h, first, fin[h, HALF:ROWS].astype(F32)), axis=0)
+
+    def beside(a, b, is_low):
+        dk = jnp.where(is_low, a, pltpu.roll(b, HEAD_DIM, 1))
+        return dk, jnp.where(is_low, pltpu.roll(a, HEAD_DIM, 1), b)
+
+    def with_level2(t):
+        base = beside(ordered_kv(2 * t), ordered_kv(2 * t + 1), low)
+        a = fin[2 * t, HOME_L2_ROW:].astype(F32)
+        b = fin[2 * t + 1, HOME_L2_ROW:].astype(F32)
+        none = jnp.zeros_like(a)
+        few_a = beside(a, none, tile_low)
+        few_b = beside(none, b, tile_low)
+        return [
+            jnp.concatenate([base[i], few_a[i], few_b[i]], axis=0).astype(BF16) for i in range(2)
+        ]
 
     def ordered_q(h, side):
         halves = []
@@ -559,13 +580,14 @@
             halves.append(jnp.concatenate([turned, x] if side else [x, turned], axis=0))
         return ordered(h, *halves)
 
+    merges = [merge_with_level2(t) for t in range(HEADS // 2)]
     loads[1].wait()
     stores = []
 
-    def store(i, parts, result):
+    def store(i, parts, left, result):
         for t, x in enumerate(parts):
             lanes = slice(t * PAIR, (t + 1) * PAIR)
-            held[i, :, lanes] = dot(merge, x.astype(BF16)).astype(BF16)
+            held[i, :, lanes] = dot(left[t], x).astype(BF16)
         stores.append(pltpu.make_async_copy(held.at[i], result, store_sem.at[i]))
         stores[-1].start()
 
@@ -574,14 +596,13 @@
         a = ordered_q(2 * t, 0)
         b = ordered_q(2 * t + 1, 1)
         both = [jnp.where(half_low, a[i], b[i]) for i in range(2)]
-        parts.append(jnp.concatenate(both, axis=0))
-    store(0, parts, dq_hbm)
+        parts.append(jnp.concatenate(both, axis=0).astype(BF16))
+    store(0, parts, [merge] * (HEADS // 2), dq_hbm)
     for load in loads[2:]:
         load.wait()
-    heads = [ordered_kv(h) for h in range(HEADS)]
-    pairs = [(heads[h], heads[h + 1]) for h in range(0, HEADS, 2)]
-    store(1, [jnp.where(low, a, pltpu.roll(b, HEAD_DIM, 1)) for a, b in pairs], dk_hbm)
-    store(2, [jnp.where(low, pltpu.roll(a, HEAD_DIM, 1), b) for a, b in pairs], dv_hbm)
+    pairs = [with_level2(t) for t in range(HEADS // 2)]
+    store(1, [pair[0] for pair in pairs], merges, dk_hbm)
+    store(2, [pair[1] for pair in pairs], merges, dv_hbm)
     for copy in stores:
         copy.wait()
 

time: 35.9 us -> 35.8 us (level)
  no operation moved by 1% of the time
where the time goes in v5:
time: 35.8 us; the launch traced here: 35.5 us
  Pallas kernels  34.9 us (97%)
  between operations  0.64 us (2%)
    pallas_call x1, Pallas kernels, local(): pl.pallas_call(kernel, out_shape=jax.ShapeDtypeStruct((HEADS, HOME_ROWS,...  32.6 us
    pallas_call x1, Pallas kernels, local(): pl.pallas_call(finish, out_shape=(one, one, one), in_specs=[hbm, hbm], ou...  2.27 us

profile of v5, /device:TPU:1, one launch (start us, length us, event | category | flops | bytes accessed | tf_op | source)
XLA Modules:
  0.0 35.5 jit_solution(6695336759976097453)
XLA Ops:
  0.6 32.6 %shard_map.76.fin_hbm = bf16[8,272,128]{2,1,0:T(8,128)(2,1)} custom-call(s32[3,8]{1,0:T(4,128)} %off_hbm.3, bf16[128,512]{1,0:T(8,128)(2,1)} %q_hbm.1, bf16[128,512]{1,0:T(8,128)(2,1)} %k_hbm.1, bf16[128,512]{1,0:T(8,128)(2,1)} %v_hbm.1, bf16[128,512]{1,0:T(8,128)(2,1)} %g_hbm.1), custom_call_target="tpu_custom_call" | custom-call | tf_op jit(solution)/shard_map/pallas_call | solution.py:617
  33.3 2.3 %shard_map.77 = (bf16[128,512]{1,0:T(8,128)(2,1)}, bf16[128,512]{1,0:T(8,128)(2,1)}, bf16[128,512]{1,0:T(8,128)(2,1)}) custom-call(s32[3,8]{1,0:T(4,128)} %off_hbm.3, bf16[8,272,128]{2,1,0:T(8,128)(2,1)} %shard_map.76.fin_hbm), custom_call_target="tpu_custom_call" | custom-call | tf_op jit(solution)/shard_map/pallas_call | solution.py:658
